TPU v7x, 256 devices: a whole 4x4x8 slice. The times are simulated.
256 devices in a mesh: dcn: 2 (over x_hi), gx: 16 (over x_lo, y, core), gy: 8 (over z).
Axes of the slice: x: 4 (x_hi: 2, x_lo: 2; x = x_hi * 2 + x_lo), y: 4, z: 8, core: 2. Of those that a mesh axis runs over, the one named last changes fastest.
Arguments:
- hidden_in: bfloat16 [262144, 5376], P(('dcn', 'gx', 'gy')), may hold values from -24 to 24
- key_cotangent: bfloat16 [262144, 1024], P(('dcn', 'gx', 'gy')), may hold values from -6 to 6
Outputs:
- key_grad: float32 [5376, 1024], P(('gx', 'gy'))
All inputs are finite; a program needn't handle non-finite values.
Results may differ from a plain program's by a relative error of at most 0.0003.
Values sent between devices are 32-bit elements; how exact they have to be, the bound alone decides.
No kernel may reach another device: no remote copies, remote signals or barrier semaphores. Data moves between devices by JAX's collectives and lax.ppermute only.
A program may use at most 128 MiB of HBM per device.

v0:
```python
import jax
import jax.numpy as jnp
from jax import lax
from jax.sharding import PartitionSpec as P

BUCKETS = 2


def body(hidden_in, key_cotangent):
    width = key_cotangent.shape[1]
    count_all = (
        hidden_in.shape[0] * lax.axis_size("dcn") * lax.axis_size("gx") * lax.axis_size("gy")
    )
    factor = jnp.float32(1.0 / count_all**0.5)
    step_cols = width // BUCKETS
    pieces = []
    for bucket in range(BUCKETS):
        cotangent = key_cotangent[:, bucket * step_cols : (bucket + 1) * step_cols]
        partial_rows = lax.psum_scatter(
            jnp.einsum("tr,tc->rc", hidden_in, cotangent, preferred_element_type=jnp.float32),
            "gx",
            scatter_dimension=0,
            tiled=True,
        )
        owned = lax.psum_scatter(partial_rows, "gy", scatter_dimension=0, tiled=True)
        pieces.append(lax.psum(owned, "dcn"))
    summed = jnp.concatenate(pieces, axis=1)
    return summed * factor


def solution(mesh):
    placed = (P(("dcn", "gx", "gy"), None), P(("dcn", "gx", "gy"), None))
    return jax.shard_map(
        body, mesh=mesh, in_specs=placed, out_specs=P(("gx", "gy"), None), check_vma=False
    )
```

profile of v0, /device:TPU:32, one launch (start us, length us, event | category | flops | bytes accessed | tf_op | source)
XLA Modules:
  0.0 263.4 jit_solution(4510531336972931567)
XLA Ops:
  6.5 0.0 reduce-scatter.7.cloned.1.call-start
  6.5 11.4 %fusion.4 = f32[5376,512]{1,0:T(8,128)} fusion(bf16[1024,5376]{1,0:T(8,128)(2,1)} %param.2, bf16[1024,1024]{1,0:T(8,128)(2,1)} %param.3), kind=kOutput, calls=%fused_computation.2 | convolution fusion | flops 5637144576 | bytes 23068672 | tf_op jit(solution)/shard_map/tr,tc->rc/dot_general | solution.py:20
  18.0 0.0 copy-start.1
  18.0 0.0 reduce-scatter.7.cloned.1.call-update
  18.0 0.0 reduce-scatter.9.cloned.1.call-start
  18.0 1.5 copy-done.1
  19.6 12.8 %fusion.2 = f32[5376,512]{1,0:T(8,128)} fusion(bf16[1024,5376]{1,0:T(8,128)(2,1)} %param.2, bf16[1024,1024]{1,0:T(8,128)(2,1)S(1)} %copy-done.1), kind=kOutput, calls=%fused_computation | convolution fusion | flops 5637144576 | bytes 23068672 | tf_op jit(solution)/shard_map/tr,tc->rc/dot_general | solution.py:20
  32.3 0.0 copy-start
  32.3 0.0 reduce-scatter.9.cloned.1.call-update
  32.3 0.0 all-reduce.8.cloned.1.call-start
  32.4 70.3 %reduce-scatter.7.cloned.1.call-done = f32[336,512]{1,0:T(8,128)} async-done(((f32[5376,512]{1,0:T(8,128)}), f32[336,512]{1,0:T(8,128)}) %reduce-scatter.7.cloned.1.call-update) | async-done | bytes 688144 | tf_op jit(solution)/shard_map/reduce_scatter | solution.py:19
  102.7 83.3 %reduce-scatter.9.cloned.1.call-done = f32[336,512]{1,0:T(8,128)} async-done(((f32[5376,512]{1,0:T(8,128)}), f32[336,512]{1,0:T(8,128)}) %reduce-scatter.9.cloned.1.call-update) | async-done | bytes 688144 | tf_op jit(solution)/shard_map/reduce_scatter | solution.py:19
  186.0 24.3 %fusion.6 = (f32[48,512]{1,0:T(8,128)S(1)}, f32[48,512]{1,0:T(8,128)S(1)}) fusion(f32[336,512]{1,0:T(8,128)} %reduce-scatter.9.cloned.1.call-done, f32[336,512]{1,0:T(8,128)} %reduce-scatter.7.cloned.1.call-done), kind=kCustom, calls=%all-reduce-scatter.2 | all-reduce-scatter fusion | flops 393217 | bytes 1573888
  210.3 3.0 %collective-permute-start = (f32[42,512]{1,0:T(8,128)S(1)}, f32[42,512]{1,0:T(8,128)S(1)}, u32[]{:S(2)}, u32[]{:S(2)}) collective-permute-start(f32[42,512]{1,0:T(8,128)S(1)} %slice.8), channel_id=1, source_target_pairs={{0,1},{1,2},{2,3},{3,4},{4,5},{5,6},{6,7},{8,9},{9,10},{10,11},{11... | collective-permute-start | bytes 258056
  213.3 0.0 copy-done
  213.3 0.6 dynamic-slice.6
  214.6 1.9 collective-permute-start.1
  216.5 0.3 collective-permute-done
  216.8 0.2 concatenate.4
  217.0 0.7 constant_dynamic-slice_fusion.1
  217.7 3.4 %collective-permute-done.1 = f32[42,512]{1,0:T(8,128)S(1)} collective-permute-done((f32[42,512]{1,0:T(8,128)S(1)}, f32[42,512]{1,0:T(8,128)S(1)}, u32[]{:S(2)}, u32[]{:S(2)}) %collective-permute-start.1) | collective-permute-done | bytes 86048
  221.1 0.2 concatenate.5
  221.3 0.7 constant_dynamic-slice_fusion
  222.0 0.0 all-reduce.8.cloned.1.call-update
  222.0 33.3 %all-reduce.8.cloned.1.call-done = (f32[42,512]{1,0:T(8,128)}, f32[42,512]{1,0:T(8,128)}) async-done(((f32[42,512]{1,0:T(8,128)}, f32[42,512]{1,0:T(8,128)}), (f32[42,512]{1,0:T(8,128)}, f32[42,512]{1,0:T(8,128)})) %all-reduce.8.cloned.1.call-update) | async-done | bytes 172048 | tf_op jit(solution)/shard_map/psum | solution.py:26
  255.2 1.6 maximum_multiply_fusion
  (2 shorter events, 0.0 us)
Async XLA Ops:
  6.5 96.2 %reduce-scatter.7.cloned.1.call-start = ((), (), s32[]{:S(2)}) async-start(), calls=%async_computation.2 | async-start | bytes 11698176 | tf_op jit(solution)/shard_map/reduce_scatter | solution.py:19
  18.0 1.6 copy-start.1
  18.0 168.0 %reduce-scatter.9.cloned.1.call-start = ((), (), s32[]{:S(2)}) async-start(), calls=%async_computation.3 | async-start | bytes 11698176 | tf_op jit(solution)/shard_map/reduce_scatter | solution.py:19
  32.3 181.0 %copy-start = (u32[256]{0:T(256)S(1)}, u32[256]{0:T(256)}, u32[]{:S(2)}) copy-start(u32[256]{0:T(256)} %constant.4) | copy-start | bytes 3076
  32.3 222.9 %all-reduce.8.cloned.1.call-start = ((), (), s32[]{:S(2)}) async-start(), calls=%async_computation.4 | async-start | bytes 393216 | tf_op jit(solution)/shard_map/psum | solution.py:26
  210.3 6.5 %collective-permute-start = (f32[42,512]{1,0:T(8,128)S(1)}, f32[42,512]{1,0:T(8,128)S(1)}, u32[]{:S(2)}, u32[]{:S(2)}) collective-permute-start(f32[42,512]{1,0:T(8,128)S(1)} %slice.8), channel_id=1, source_target_pairs={{0,1},{1,2},{2,3},{3,4},{4,5},{5,6},{6,7},{8,9},{9,10},{10,11},{11... | collective-permute-start | bytes 258056
  214.6 6.5 %collective-permute-start.1 = (f32[42,512]{1,0:T(8,128)S(1)}, f32[42,512]{1,0:T(8,128)S(1)}, u32[]{:S(2)}, u32[]{:S(2)}) collective-permute-start(f32[42,512]{1,0:T(8,128)S(1)} %slice.9), channel_id=1, source_target_pairs={{0,1},{1,2},{2,3},{3,4},{4,5},{5,6},{6,7},{8,9},{9,10},{10,11},{11... | collective-permute-start | bytes 258056
Sparse Core Ops, SparseCore 0:
  18.1 84.5 reduce-scatter.6
  105.3 80.7 reduce-scatter.8
  222.1 33.0 all-reduce.7
where the time goes:
time: 264 us; the launch traced here: 263 us
  waiting for transfers between devices  191 us (72%)
  blocking collectives  24.3 us (9%)
  matrix products  24.2 us (9%)
  between operations  13.8 us (5%)
  starting transfers between devices  4.98 us (2%)
  local copies, waits for them, and re-layouts  3.85 us (1%)
    reduce_scatter x2, waiting for transfers between devices, body(): lax.psum_scatter(jnp.einsum('tr,tc->rc', hidden_in, cotangent, preferred_...  154 us
    psum x1, waiting for transfers between devices, body(): pieces.append(lax.psum(owned, 'dcn'))  33.3 us
    unnamed x1, blocking collectives  24.3 us
    dot_general x2, matrix products, body(): jnp.einsum('tr,tc->rc', hidden_in, cotangent, preferred_element_type=jnp....  24.2 us
  transfers between devices with their start and end apart: 5, of which 5 were waited for; matrix products, arithmetic and copies ran while one was open for 5% of the time, Pallas kernels for 0%

commit v1 on v0

v1 whole, which is shorter than its diff:
```python
import jax
import jax.numpy as jnp
from jax import lax
from jax.experimental import pallas as pl
from jax.experimental.pallas import tpu as pltpu
from jax.sharding import PartitionSpec as P

AXES = ("dcn", "gx", "gy")
ROWS = 7
STEP = 256

OFF_X = (320, 80, 0, 112)
OFF_Y = (352, 144, 32, 176)
OFF_Z = (304, 272, 240, 208, 64, 224, 256, 288)
CUT1, CUT2, UNITS = 80, 240, 384


def pick(table, k):
    value = jnp.int32(table[0])
    for i in range(1, len(table)):
        value = jnp.where(k == i, jnp.int32(table[i]), value)
    return value


def coords():
    dcn, gx, gy = (lax.axis_index(a) for a in AXES)
    core = lax.rem(gx, 2)
    y = lax.rem(lax.div(gx, 2), 4)
    x = dcn * 2 + lax.div(gx, 8)
    return x, y, gy, core


def grad_kernel(where_ref, h_ref, c_ref, keep, send1, send2, send3, acc, sem):
    i = pl.program_id(0)
    x, y, z, core = where_ref[0], where_ref[1], where_ref[2], where_ref[3]
    prod = lax.dot_general(
        h_ref[...], c_ref[...], (((0,), (0,)), ((), ())), preferred_element_type=jnp.float32
    )
    flat = acc.reshape(5376 * 8, 128)
    for s in range(8):
        flat[pl.ds(i * (STEP * 8) + s, STEP, stride=8), :] = prod[:, s * 128 : (s + 1) * 128]

    parts = acc.reshape(16, 8, 2, 3, ROWS * 8, 128)
    done = lax.div((i + 1) * STEP, 336)
    before = lax.div(i * STEP, 336)

    def copy_out(src, unit, count, mine):
        def put(dst, base):
            pltpu.make_async_copy(src, dst.at[pl.ds(unit - base, count)], sem).start()

        pl.when(mine)(lambda: put(keep, 0))
        pl.when(jnp.logical_not(mine) & (unit < CUT1))(lambda: put(send1, 0))
        pl.when(jnp.logical_not(mine) & (unit >= CUT1) & (unit < CUT2))(lambda: put(send2, CUT1))
        pl.when(jnp.logical_not(mine) & (unit >= CUT2))(lambda: put(send3, CUT2))

    @pl.when(done > before)
    def _():
        b = done - 1
        c2 = lax.rem(b, 2)
        y2 = lax.rem(lax.div(b, 2), 4)
        xl = lax.div(b, 8)
        sign = 1 - 2 * c2
        mine = c2 == core
        rely = lax.rem(sign * (y2 - y) + 4, 4)
        for xh in range(2):
            relx = lax.rem(sign * (2 * xh + xl - x) + 4, 4)
            copy_out(parts.at[b, :, xh, 0], pick(OFF_X, relx) + rely * 8, 8, mine)
            copy_out(parts.at[b, :, xh, 1], pick(OFF_Y, rely) + (xl * 2 + xh) * 8, 8, mine)
        for z2 in range(8):
            relz = lax.rem(sign * (z2 - z) + 8, 8)
            copy_out(parts.at[b, z2, :, 2], pick(OFF_Z, relz) + rely * 4 + xl * 2, 2, mine)

    @pl.when(i == pl.num_programs(0) - 1)
    def _():
        for out in (keep, send1, send2, send3):
            pltpu.make_async_copy(out, out, sem).wait()


def local_grad(where, hidden_in, key_cotangent):
    tokens, width = hidden_in.shape
    keys = key_cotangent.shape[1]
    shape = lambda n: jax.ShapeDtypeStruct((n, ROWS * 8, 128), jnp.float32)
    anywhere = pl.BlockSpec(memory_space=pl.ANY)
    return pl.pallas_call(
        grad_kernel,
        out_shape=(shape(UNITS), shape(CUT1), shape(CUT2 - CUT1), shape(UNITS - CUT2)),
        grid_spec=pltpu.PrefetchScalarGridSpec(
            num_scalar_prefetch=1,
            grid=(width // STEP,),
            in_specs=[
                pl.BlockSpec((tokens, STEP), lambda i, w: (0, i)),
                pl.BlockSpec((tokens, keys), lambda i, w: (0, 0)),
            ],
            out_specs=(anywhere,) * 4,
            scratch_shapes=[
                pltpu.VMEM((768, ROWS * 8, 128), jnp.float32),
                pltpu.SemaphoreType.DMA,
            ],
        ),
        compiler_params=pltpu.CompilerParams(vmem_limit_bytes=48 * 1024 * 1024),
        cost_estimate=pl.CostEstimate(
            flops=2 * tokens * width * keys,
            bytes_accessed=2 * tokens * (width + keys) + 4 * width * keys,
            transcendentals=0,
        ),
        name="local_grad",
    )(where, hidden_in, key_cotangent)


def moves(axis, hop, both=True):
    pairs = []
    for x in range(4):
        for y in range(4):
            for z in range(8):
                for c in range(2):
                    at = [x, y, z]
                    d = hop if c == 0 or not both else -hop
                    at[axis] = (at[axis] + d) % (4, 4, 8)[axis]
                    pairs.append((place(x, y, z, c), place(*at, c)))
    return pairs


def place(x, y, z, c):
    return (x // 2) * 128 + (((x % 2) * 4 + y) * 2 + c) * 8 + z


SWAP = [(place(x, y, z, c), place(x, y, z, 1 - c)) for x in range(4) for y in range(4) for z in range(8) for c in range(2)]


def go(a, axis, hop):
    return lax.ppermute(a, AXES, moves(axis, hop))


def body(hidden_in, key_cotangent):
    count_all = (
        hidden_in.shape[0] * lax.axis_size("dcn") * lax.axis_size("gx") * lax.axis_size("gy")
    )
    factor = jnp.float32(1.0 / count_all**0.5)
    x, y, z, core = coords()
    sign = 1 - 2 * core
    where = jnp.stack([x, y, z, core]).astype(jnp.int32)
    keep, send1, send2, send3 = local_grad(where, hidden_in, key_cotangent)
    got1 = lax.ppermute(send1, AXES, SWAP)
    got2 = lax.ppermute(send2, AXES, SWAP)
    got3 = lax.ppermute(send3, AXES, SWAP)

    def own(unit, count):
        mine = keep[unit : unit + count]
        if unit < CUT1:
            return mine + got1[unit : unit + count]
        if unit < CUT2:
            return mine + got2[unit - CUT1 : unit - CUT1 + count]
        return mine + got3[unit - CUT2 : unit - CUT2 + count]

    def ring4(off, axis):
        a = go(own(off[2], 32), axis, 1)
        b = go(own(off[3], 32), axis, -1)
        a = go(a + own(off[1], 32), axis, 1)
        return a + b + own(off[0], 32)

    def ring8(off, axis):
        a = go(own(off[4], 16), axis, 1)
        b = go(own(off[5], 16), axis, -1)
        a = go(a + own(off[3], 16), axis, 1)
        b = go(b + own(off[6], 16), axis, -1)
        a = go(a + own(off[2], 16), axis, 1)
        b = go(b + own(off[7], 16), axis, -1)
        a = go(a + own(off[1], 16), axis, 1)
        return a + b + own(off[0], 16)

    part_z = ring8(OFF_Z, 2)
    part_x = ring4(OFF_X, 0)
    part_y = ring4(OFF_Y, 1)

    def direct_y(part, n):
        one = go(part[n : 2 * n], 1, 1)
        back = go(part[3 * n :], 1, -1)
        far = go(part[2 * n : 3 * n], 1, 2)
        return part[:n] + one + back + far

    def along_z(part):
        def at(k):
            return lax.dynamic_index_in_dim(part, lax.rem(z + sign * k + 16, 8), axis=-3, keepdims=True)

        up = go(jnp.concatenate([at(4), at(3)], -3), 2, 2)
        down = go(jnp.concatenate([at(-3), at(-2)], -3), 2, -2)
        a2 = go(up[..., :1, :, :] + at(2), 2, 2)
        a1 = go(up[..., 1:, :, :] + at(1), 2, 1)
        b1 = go(down[..., :1, :, :] + at(-1), 2, -1)
        return (at(0) + down[..., 1:, :, :] + a2 + a1 + b1)[..., 0, :, :]

    part_x = along_z(direct_y(part_x, 8))
    part_z = direct_y(part_z, 4)
    part_y = along_z(part_y.reshape(4, 8, ROWS * 8, 128))

    both = jnp.stack([part_y.reshape(2, 2, ROWS * 8, 128), part_z.reshape(2, 2, ROWS * 8, 128)], axis=2)
    xl = lax.rem(x, 2)
    mine = lax.dynamic_index_in_dim(both, xl, keepdims=False)
    other = lax.dynamic_index_in_dim(both, 1 - xl, keepdims=False)
    both = mine + go(mine, 0, 2) + go(other, 0, 1) + go(other, 0, -1)
    partner = go(part_x, 0, 2)
    first = x < 2
    part_x = jnp.stack([jnp.where(first, part_x, partner), jnp.where(first, partner, part_x)])
    result = jnp.concatenate([part_x[:, None], both], axis=1)
    return result.reshape(2 * 3 * ROWS, 1024) * factor


def solution(mesh):
    placed = (P(AXES, None), P(AXES, None))
    return jax.shard_map(
        body, mesh=mesh, in_specs=placed, out_specs=P(("gx", "gy"), None), check_vma=False
    )
```

time: 264 us -> 168 us (0.64)
  waiting for transfers between devices: 191 us -> 61 us
  starting transfers between devices: 4.98 us -> 58.8 us
  Pallas kernels: 0 us -> 26.4 us
  blocking collectives: 24.3 us -> 0 us
  matrix products: 24.2 us -> 0 us
  other arithmetic: 1.63 us -> 16.9 us
  between operations: 13.8 us -> 0.18 us
    reduce_scatter x2 -> x0, waiting for transfers between devices: 154 us -> none  [body(): lax.psum_scatter(jnp.einsum('tr,tc->rc', hidden_in, cotangent, preferred_...]
    ppermute x0 -> x36, waiting for transfers between devices: none -> 61 us  [the longest x33 44.7 us: go(): return lax.ppermute(a, AXES, moves(axis, hop))]
    ppermute x0 -> x36, starting transfers between devices: none -> 58.8 us  [the longest x33 58.2 us: go(): return lax.ppermute(a, AXES, moves(axis, hop))]
    psum x1 -> x0, waiting for transfers between devices: 33.3 us -> none  [body(): pieces.append(lax.psum(owned, 'dcn'))]
    pallas_call x0 -> x1, Pallas kernels: none -> 26.4 us  [local_grad(): pl.pallas_call(grad_kernel, out_shape=(shape(UNITS), shape(CUT1), shape(C...]
    unnamed x1 -> x0, blocking collectives: 24.3 us -> none
    dot_general x2 -> x0, matrix products: 24.2 us -> none  [body(): jnp.einsum('tr,tc->rc', hidden_in, cotangent, preferred_element_type=jnp....]
    add x0 -> x14, other arithmetic: none -> 16.7 us  [the longest x2 6.05 us: own(): return mine + got2[unit - CUT1:unit - CUT1 + count]]
  transfers between devices with their start and end apart: 5 -> 36, of which waited for: 5 -> 10; matrix products, arithmetic and copies ran while one was open for 5% -> 10% of each run, Pallas kernels for 0% -> 0%
where the time goes in v1:
time: 168 us; the launch traced here: 166 us
  waiting for transfers between devices  61 us (36%)
  starting transfers between devices  58.8 us (35%)
  Pallas kernels  26.4 us (16%)
  other arithmetic  16.9 us (10%)
  local copies, waits for them, and re-layouts  2.44 us (1%)
    ppermute x33, starting transfers between devices, go(): return lax.ppermute(a, AXES, moves(axis, hop))  58.2 us
    ppermute x33, waiting for transfers between devices, go(): return lax.ppermute(a, AXES, moves(axis, hop))  44.7 us
    pallas_call x1, Pallas kernels, local_grad(): pl.pallas_call(grad_kernel, out_shape=(shape(UNITS), shape(CUT1), shape(C...  26.4 us
    ppermute x1, waiting for transfers between devices, body(): got1 = lax.ppermute(send1, AXES, SWAP)  16.3 us
    add x2, other arithmetic, own(): return mine + got2[unit - CUT1:unit - CUT1 + count]  6.05 us
  transfers between devices with their start and end apart: 36, of which 10 were waited for; matrix products, arithmetic and copies ran while one was open for 10% of the time, Pallas kernels for 0%

profile of v1, /device:TPU:32, one launch (start us, length us, event | category | flops | bytes accessed | tf_op | source)
XLA Modules:
  0.0 165.7 jit_solution(16929944741761482535)
XLA Ops:
  0.1 1.6 copy-done
  1.7 26.4 %local_grad.1 = (f32[384,56,128]{2,1,0:T(8,128)}, f32[80,56,128]{2,1,0:T(8,128)S(1)}, f32[160,56,128]{2,1,0:T(8,128)}, f32[144,56,128]{2,1,0:T(8,128)}) custom-call(s32[4]{0:T(128)S(1)} %pad_add_fusion.where_ref, bf16[1024,5376]{1,0:T(8,128)(2,1)} %h_ref.1, bf16[1024,1024]{1,0:T(8,128)(2,1)S(1)} %copy-done), custom_call_target="tpu_custom_call" | custom-call | flops 11274289152 | bytes 35127296 | tf_op jit(solution)/shard_map/local_grad/pallas_call | solution.py:84
  28.8 16.3 %collective-permute-done = f32[80,56,128]{2,1,0:T(8,128)S(1)} collective-permute-done((f32[80,56,128]{2,1,0:T(8,128)S(1)}, f32[80,56,128]{2,1,0:T(8,128)S(1)}, u32[]{:S(2)}, u32[]{:S(2)}) %collective-permute-start) | collective-permute-done | bytes 2293792 | tf_op jit(solution)/shard_map/ppermute | solution.py:143
  45.1 1.7 %slice_add_fusion.7 = (f32[32,56,128]{2,1,0:T(8,128)S(1)}, f32[32,56,128]{2,1,0:T(8,128)S(1)}) fusion(f32[80,56,128]{2,1,0:T(8,128)S(1)} %collective-permute-done, f32[384,56,128]{2,1,0:T(8,128)} %get-tuple-element.9), kind=kLoop, calls=%fused_computation.11 | loop fusion | flops 458752 | bytes 5505024 | tf_op jit(solution)/shard_map/add | solution.py:150
  48.1 1.8 %collective-permute-start.15 = (f32[32,56,128]{2,1,0:T(8,128)S(1)}, f32[32,56,128]{2,1,0:T(8,128)S(1)}, u32[]{:S(2)}, u32[]{:S(2)}) collective-permute-start(f32[32,56,128]{2,1,0:T(8,128)S(1)} %get-tuple-element.26), channel_id=1, source_target_pairs={{0,16},{8,56},{1,17},{9,57},{2,18},{10,58},{3,19},{11,59},{4,20},{... | collective-permute-start | bytes 2752520 | tf_op jit(solution)/shard_map/ppermute | solution.py:131
  50.9 2.0 %collective-permute-start.23 = (f32[16,56,128]{2,1,0:T(8,128)S(1)}, f32[16,56,128]{2,1,0:T(8,128)S(1)}, u32[]{:S(2)}, u32[]{:S(2)}) collective-permute-start(f32[16,56,128]{2,1,0:T(8,128)S(1)} %slice_add_fusion.15), channel_id=1, source_target_pairs={{0,1},{8,15},{1,2},{9,8},{2,3},{10,9},{3,4},{11,10},{4,5},{12,11},... | collective-permute-start | bytes 1376264 | tf_op jit(solution)/shard_map/ppermute | solution.py:131
  52.9 6.6 %collective-permute-done.23 = f32[16,56,128]{2,1,0:T(8,128)S(1)} collective-permute-done((f32[16,56,128]{2,1,0:T(8,128)S(1)}, f32[16,56,128]{2,1,0:T(8,128)S(1)}, u32[]{:S(2)}, u32[]{:S(2)}) %collective-permute-start.23) | collective-permute-done | bytes 458784 | tf_op jit(solution)/shard_map/ppermute | solution.py:131
  59.5 2.1 %slice_add_fusion.11 = (f32[16,56,128]{2,1,0:T(8,128)S(1)}, f32[16,56,128]{2,1,0:T(8,128)}) fusion(f32[160,56,128]{2,1,0:T(8,128)S(1)} %collective-permute-done.2, f32[384,56,128]{2,1,0:T(8,128)} %get-tuple-element.9, f32[16,56,128]{2,1,0:T(8,128)S(1)} %collective-permute-done.23), kind=kLoop, calls=%fused_computation.18 | loop fusion | flops 344064 | bytes 3211264 | tf_op jit(solution)/shard_map/add | solution.py:152
  61.6 3.9 %collective-permute-start.27 = (f32[16,56,128]{2,1,0:T(8,128)S(1)}, f32[16,56,128]{2,1,0:T(8,128)S(1)}, u32[]{:S(2)}, u32[]{:S(2)}) collective-permute-start(f32[16,56,128]{2,1,0:T(8,128)S(1)} %get-tuple-element.17), channel_id=1, source_target_pairs={{0,7},{8,9},{1,0},{9,10},{2,1},{10,11},{3,2},{11,12},{4,3},{12,13}... | collective-permute-start | bytes 1376264 | tf_op jit(solution)/shard_map/ppermute | solution.py:131
  65.5 4.0 %slice_add_fusion.5 = (f32[32,56,128]{2,1,0:T(8,128)}, f32[32,56,128]{2,1,0:T(8,128)}, f32[32,56,128]{2,1,0:T(8,128)S(1)}, f32[32,56,128]{2,1,0:T(8,128)S(1)}) fusion(f32[160,56,128]{2,1,0:T(8,128)S(1)} %collective-permute-done.2, f32[384,56,128]{2,1,0:T(8,128)} %get-tuple-element.9, f32[32,56,128]{2,1,0:T(8,128)S(1)} %collective-permute-done.15, ...), kind=kLoop, calls=%fused_computation.8 | loop fusion | flops 1376256 | bytes 12845056 | tf_op jit(solution)/shard_map/add | solution.py:152
  69.5 1.7 %collective-permute-start.4 = (f32[32,56,128]{2,1,0:T(8,128)}, f32[32,56,128]{2,1,0:T(8,128)S(1)}, u32[]{:S(2)}, u32[]{:S(2)}) collective-permute-start(f32[32,56,128]{2,1,0:T(8,128)} %get-tuple-element.13), channel_id=1, source_target_pairs={{0,192},{8,72},{1,193},{9,73},{2,194},{10,74},{3,195},{11,75},{4,1... | collective-permute-start | bytes 2752520 | tf_op jit(solution)/shard_map/ppermute | solution.py:131
  71.2 1.7 %collective-permute-start.17 = (f32[32,56,128]{2,1,0:T(8,128)}, f32[32,56,128]{2,1,0:T(8,128)}, u32[]{:S(2)}, u32[]{:S(2)}) collective-permute-start(f32[32,56,128]{2,1,0:T(8,128)} %get-tuple-element.14), channel_id=1, source_target_pairs={{0,48},{8,24},{1,49},{9,25},{2,50},{10,26},{3,51},{11,27},{4,52},{... | collective-permute-start | bytes 2752520 | tf_op jit(solution)/shard_map/ppermute | solution.py:131
  73.6 8.8 %collective-permute-done.24 = f32[16,56,128]{2,1,0:T(8,128)} collective-permute-done((f32[16,56,128]{2,1,0:T(8,128)}, f32[16,56,128]{2,1,0:T(8,128)}, u32[]{:S(2)}, u32[]{:S(2)}) %collective-permute-start.24) | collective-permute-done | bytes 458784 | tf_op jit(solution)/shard_map/ppermute | solution.py:131
  82.4 1.7 %fusion.6 = (f32[16,56,128]{2,1,0:T(8,128)S(1)}, f32[16,56,128]{2,1,0:T(8,128)S(1)}) fusion(f32[16,56,128]{2,1,0:T(8,128)S(1)} %collective-permute-done.27, f32[144,56,128]{2,1,0:T(8,128)} %collective-permute-done.5, f32[384,56,128]{2,1,0:T(8,128)} %get-tuple-element.9, f32[16,56,128]{2,1,0:T(8,128)} %collective-permute-done.24), kind=kLoop, calls=%fused_computation.17 | loop fusion | flops 458752 | bytes 3670016 | tf_op jit(solution)/shard_map/add | solution.py:165
  84.1 3.3 %collective-permute-start.28 = (f32[16,56,128]{2,1,0:T(8,128)S(1)}, f32[16,56,128]{2,1,0:T(8,128)S(1)}, u32[]{:S(2)}, u32[]{:S(2)}) collective-permute-start(f32[16,56,128]{2,1,0:T(8,128)S(1)} %get-tuple-element.23), channel_id=1, source_target_pairs={{0,7},{8,9},{1,0},{9,10},{2,1},{10,11},{3,2},{11,12},{4,3},{12,13}... | collective-permute-start | bytes 1376264 | tf_op jit(solution)/shard_map/ppermute | solution.py:131
  87.4 4.8 %collective-permute-done.4 = f32[32,56,128]{2,1,0:T(8,128)S(1)} collective-permute-done((f32[32,56,128]{2,1,0:T(8,128)}, f32[32,56,128]{2,1,0:T(8,128)S(1)}, u32[]{:S(2)}, u32[]{:S(2)}) %collective-permute-start.4) | collective-permute-done | bytes 917536 | tf_op jit(solution)/shard_map/ppermute | solution.py:131
  92.6 3.2 %fusion.2 = (f32[32,56,128]{2,1,0:T(8,128)S(1)}, f32[32,56,128]{2,1,0:T(8,128)S(1)}) fusion(f32[144,56,128]{2,1,0:T(8,128)} %collective-permute-done.5, f32[384,56,128]{2,1,0:T(8,128)} %get-tuple-element.9, f32[32,56,128]{2,1,0:T(8,128)} %collective-permute-done.3, f32[32,56,128]{2,1,0:T(8,128)S(1)} %collective-permute-done.4, ...), kind=kLoop, calls=%fused_computation.7 | loop fusion | flops 1376256 | bytes 9175040 | tf_op jit(solution)/shard_map/add | solution.py:159
  96.7 3.4 %collective-permute-start.8 = (f32[8,56,128]{2,1,0:T(8,128)S(1)}, f32[8,56,128]{2,1,0:T(8,128)S(1)}, u32[]{:S(2)}, u32[]{:S(2)}) collective-permute-start(f32[8,56,128]{2,1,0:T(8,128)S(1)} %get-tuple-element.30), channel_id=1, source_target_pairs={{0,32},{8,40},{1,33},{9,41},{2,34},{10,42},{3,35},{11,43},{4,36},{... | collective-permute-start | bytes 688136 | tf_op jit(solution)/shard_map/ppermute | solution.py:131
  100.2 8.3 %collective-permute-done.6 = f32[8,56,128]{2,1,0:T(8,128)S(1)} collective-permute-done((f32[8,56,128]{2,1,0:T(8,128)S(1)}, f32[8,56,128]{2,1,0:T(8,128)S(1)}, u32[]{:S(2)}, u32[]{:S(2)}) %collective-permute-start.6) | collective-permute-done | bytes 229408 | tf_op jit(solution)/shard_map/ppermute | solution.py:131
  108.5 3.7 %collective-permute-start.18 = (f32[4,2,56,128]{3,2,1,0:T(8,128)S(1)}, f32[4,2,56,128]{3,2,1,0:T(8,128)S(1)}, u32[]{:S(2)}, u32[]{:S(2)}) collective-permute-start(f32[4,2,56,128]{3,2,1,0:T(8,128)S(1)} %pad_maximum_fusion), channel_id=1, source_target_pairs={{0,6},{8,10},{1,7},{9,11},{2,0},{10,12},{3,1},{11,13},{4,2},{12,14... | collective-permute-start | bytes 688136 | tf_op jit(solution)/shard_map/ppermute | solution.py:131
  112.2 2.4 %collective-permute-start.19 = (f32[4,2,56,128]{3,2,1,0:T(8,128)S(1)}, f32[4,2,56,128]{3,2,1,0:T(8,128)S(1)}, u32[]{:S(2)}, u32[]{:S(2)}) collective-permute-start(f32[4,2,56,128]{3,2,1,0:T(8,128)S(1)} %pad_maximum_fusion.1), channel_id=1, source_target_pairs={{0,2},{8,14},{1,3},{9,15},{2,4},{10,8},{3,5},{11,9},{4,6},{12,10},... | collective-permute-start | bytes 688136 | tf_op jit(solution)/shard_map/ppermute | solution.py:131
  114.7 1.8 %collective-permute-start.9 = (f32[2,56,128]{2,1,0:T(8,128)S(1)}, f32[2,56,128]{2,1,0:T(8,128)S(1)}, u32[]{:S(2)}, u32[]{:S(2)}) collective-permute-start(f32[2,56,128]{2,1,0:T(8,128)S(1)} %pad_maximum_fusion.2), channel_id=1, source_target_pairs={{0,6},{8,10},{1,7},{9,11},{2,0},{10,12},{3,1},{11,13},{4,2},{12,14... | collective-permute-start | bytes 172040 | tf_op jit(solution)/shard_map/ppermute | solution.py:131
  116.6 2.5 %collective-permute-start.10 = (f32[2,56,128]{2,1,0:T(8,128)S(1)}, f32[2,56,128]{2,1,0:T(8,128)S(1)}, u32[]{:S(2)}, u32[]{:S(2)}) collective-permute-start(f32[2,56,128]{2,1,0:T(8,128)S(1)} %pad_maximum_fusion.3), channel_id=1, source_target_pairs={{0,2},{8,14},{1,3},{9,15},{2,4},{10,8},{3,5},{11,9},{4,6},{12,10},... | collective-permute-start | bytes 172040 | tf_op jit(solution)/shard_map/ppermute | solution.py:131
  121.9 7.0 %collective-permute-start.26 = (f32[16,56,128]{2,1,0:T(8,128)S(1)}, f32[16,56,128]{2,1,0:T(8,128)S(1)}, u32[]{:S(2)}, u32[]{:S(2)}) collective-permute-start(f32[16,56,128]{2,1,0:T(8,128)S(1)} %get-tuple-element.22), channel_id=1, source_target_pairs={{0,1},{8,15},{1,2},{9,8},{2,3},{10,9},{3,4},{11,10},{4,5},{12,11},... | collective-permute-start | bytes 1376264 | tf_op jit(solution)/shard_map/ppermute | solution.py:131
  128.9 2.1 %collective-permute-start.11 = (f32[1,56,128]{2,1,0:T(8,128)S(1)}, f32[1,56,128]{2,1,0:T(8,128)S(1)}, u32[]{:S(2)}, u32[]{:S(2)}) collective-permute-start(f32[1,56,128]{2,1,0:T(8,128)S(1)} %get-tuple-element.40), channel_id=1, source_target_pairs={{0,2},{8,14},{1,3},{9,15},{2,4},{10,8},{3,5},{11,9},{4,6},{12,10},... | collective-permute-start | bytes 86024 | tf_op jit(solution)/shard_map/ppermute | solution.py:131
  133.1 3.4 %collective-permute-done.11 = f32[1,56,128]{2,1,0:T(8,128)S(1)} collective-permute-done((f32[1,56,128]{2,1,0:T(8,128)S(1)}, f32[1,56,128]{2,1,0:T(8,128)S(1)}, u32[]{:S(2)}, u32[]{:S(2)}) %collective-permute-start.11) | collective-permute-done | bytes 28704 | tf_op jit(solution)/shard_map/ppermute | solution.py:131
  136.5 2.8 %collective-permute-start.20 = (f32[4,1,56,128]{3,2,1,0:T(8,128)S(1)}, f32[4,1,56,128]{3,2,1,0:T(8,128)S(1)}, u32[]{:S(2)}, u32[]{:S(2)}) collective-permute-start(f32[4,1,56,128]{3,2,1,0:T(8,128)S(1)} %get-tuple-element.27), channel_id=1, source_target_pairs={{0,2},{8,14},{1,3},{9,15},{2,4},{10,8},{3,5},{11,9},{4,6},{12,10},... | collective-permute-start | bytes 344072 | tf_op jit(solution)/shard_map/ppermute | solution.py:131
  139.3 3.3 %collective-permute-start.21 = (f32[4,1,56,128]{3,2,1,0:T(8,128)S(1)}, f32[4,1,56,128]{3,2,1,0:T(8,128)S(1)}, u32[]{:S(2)}, u32[]{:S(2)}) collective-permute-start(f32[4,1,56,128]{3,2,1,0:T(8,128)S(1)} %get-tuple-element.28), channel_id=1, source_target_pairs={{0,1},{8,15},{1,2},{9,8},{2,3},{10,9},{3,4},{11,10},{4,5},{12,11},... | collective-permute-start | bytes 344072 | tf_op jit(solution)/shard_map/ppermute | solution.py:131
  145.5 2.9 %collective-permute-start.32 = (f32[4,56,128]{2,1,0:T(8,128)S(1)}, f32[4,56,128]{2,1,0:T(8,128)S(1)}, u32[]{:S(2)}, u32[]{:S(2)}) collective-permute-start(f32[4,56,128]{2,1,0:T(8,128)S(1)} %get-tuple-element.38), channel_id=1, source_target_pairs={{0,32},{8,40},{1,33},{9,41},{2,34},{10,42},{3,35},{11,43},{4,36},{... | collective-permute-start | bytes 344072 | tf_op jit(solution)/shard_map/ppermute | solution.py:131
  148.9 6.1 %collective-permute-done.30 = f32[4,56,128]{2,1,0:T(8,128)S(1)} collective-permute-done((f32[4,56,128]{2,1,0:T(8,128)S(1)}, f32[4,56,128]{2,1,0:T(8,128)S(1)}, u32[]{:S(2)}, u32[]{:S(2)}) %collective-permute-start.30) | collective-permute-done | bytes 114720 | tf_op jit(solution)/shard_map/ppermute | solution.py:131
  157.2 1.6 collective-permute-start.33
  158.7 5.8 %collective-permute-done.33 = f32[2,2,56,128]{3,2,1,0:T(8,128)S(1)} collective-permute-done((f32[2,2,56,128]{3,2,1,0:T(8,128)S(1)}, f32[2,2,56,128]{3,2,1,0:T(8,128)S(1)}, u32[]{:S(2)}, u32[]{:S(2)}) %collective-permute-start.33) | collective-permute-done | bytes 114720 | tf_op jit(solution)/shard_map/ppermute | solution.py:131
  (72 shorter events, 17.0 us)
Async XLA Ops:
  28.1 31.4 %collective-permute-start.2 = (f32[160,56,128]{2,1,0:T(8,128)}, f32[160,56,128]{2,1,0:T(8,128)S(1)}, u32[]{:S(2)}, u32[]{:S(2)}) collective-permute-start(f32[160,56,128]{2,1,0:T(8,128)} %get-tuple-element.11), channel_id=1, source_target_pairs={{0,8},{8,0},{1,9},{9,1},{2,10},{10,2},{3,11},{11,3},{4,12},{12,4},... | collective-permute-start | bytes 13762568 | tf_op jit(solution)/shard_map/ppermute | solution.py:144
  28.2 45.1 %collective-permute-start.5 = (f32[144,56,128]{2,1,0:T(8,128)}, f32[144,56,128]{2,1,0:T(8,128)}, u32[]{:S(2)}, u32[]{:S(2)}) collective-permute-start(f32[144,56,128]{2,1,0:T(8,128)} %get-tuple-element.12), channel_id=1, source_target_pairs={{0,8},{8,0},{1,9},{9,1},{2,10},{10,2},{3,11},{11,3},{4,12},{12,4},... | collective-permute-start | bytes 12386312 | tf_op jit(solution)/shard_map/ppermute | solution.py:145
  28.7 16.4 %collective-permute-start = (f32[80,56,128]{2,1,0:T(8,128)S(1)}, f32[80,56,128]{2,1,0:T(8,128)S(1)}, u32[]{:S(2)}, u32[]{:S(2)}) collective-permute-start(f32[80,56,128]{2,1,0:T(8,128)S(1)} %get-tuple-element.10), channel_id=1, source_target_pairs={{0,8},{8,0},{1,9},{9,1},{2,10},{10,2},{3,11},{11,3},{4,12},{12,4},... | collective-permute-start | bytes 6881288 | tf_op jit(solution)/shard_map/ppermute | solution.py:143
  46.8 18.8 %collective-permute-start.1 = (f32[32,56,128]{2,1,0:T(8,128)S(1)}, f32[32,56,128]{2,1,0:T(8,128)S(1)}, u32[]{:S(2)}, u32[]{:S(2)}) collective-permute-start(f32[32,56,128]{2,1,0:T(8,128)S(1)} %get-tuple-element.25), channel_id=1, source_target_pairs={{0,64},{8,200},{1,65},{9,201},{2,66},{10,202},{3,67},{11,203},{4,6... | collective-permute-start | bytes 2752520 | tf_op jit(solution)/shard_map/ppermute | solution.py:131
  48.1 17.5 %collective-permute-start.15 = (f32[32,56,128]{2,1,0:T(8,128)S(1)}, f32[32,56,128]{2,1,0:T(8,128)S(1)}, u32[]{:S(2)}, u32[]{:S(2)}) collective-permute-start(f32[32,56,128]{2,1,0:T(8,128)S(1)} %get-tuple-element.26), channel_id=1, source_target_pairs={{0,16},{8,56},{1,17},{9,57},{2,18},{10,58},{3,19},{11,59},{4,20},{... | collective-permute-start | bytes 2752520 | tf_op jit(solution)/shard_map/ppermute | solution.py:131
  50.9 8.6 %collective-permute-start.23 = (f32[16,56,128]{2,1,0:T(8,128)S(1)}, f32[16,56,128]{2,1,0:T(8,128)S(1)}, u32[]{:S(2)}, u32[]{:S(2)}) collective-permute-start(f32[16,56,128]{2,1,0:T(8,128)S(1)} %slice_add_fusion.15), channel_id=1, source_target_pairs={{0,1},{8,15},{1,2},{9,8},{2,3},{10,9},{3,4},{11,10},{4,5},{12,11},... | collective-permute-start | bytes 1376264 | tf_op jit(solution)/shard_map/ppermute | solution.py:131
  61.6 12.0 %collective-permute-start.27 = (f32[16,56,128]{2,1,0:T(8,128)S(1)}, f32[16,56,128]{2,1,0:T(8,128)S(1)}, u32[]{:S(2)}, u32[]{:S(2)}) collective-permute-start(f32[16,56,128]{2,1,0:T(8,128)S(1)} %get-tuple-element.17), channel_id=1, source_target_pairs={{0,7},{8,9},{1,0},{9,10},{2,1},{10,11},{3,2},{11,12},{4,3},{12,13}... | collective-permute-start | bytes 1376264 | tf_op jit(solution)/shard_map/ppermute | solution.py:131
  69.5 22.6 %collective-permute-start.4 = (f32[32,56,128]{2,1,0:T(8,128)}, f32[32,56,128]{2,1,0:T(8,128)S(1)}, u32[]{:S(2)}, u32[]{:S(2)}) collective-permute-start(f32[32,56,128]{2,1,0:T(8,128)} %get-tuple-element.13), channel_id=1, source_target_pairs={{0,192},{8,72},{1,193},{9,73},{2,194},{10,74},{3,195},{11,75},{4,1... | collective-permute-start | bytes 2752520 | tf_op jit(solution)/shard_map/ppermute | solution.py:131
  71.2 20.9 %collective-permute-start.17 = (f32[32,56,128]{2,1,0:T(8,128)}, f32[32,56,128]{2,1,0:T(8,128)}, u32[]{:S(2)}, u32[]{:S(2)}) collective-permute-start(f32[32,56,128]{2,1,0:T(8,128)} %get-tuple-element.14), channel_id=1, source_target_pairs={{0,48},{8,24},{1,49},{9,25},{2,50},{10,26},{3,51},{11,27},{4,52},{... | collective-permute-start | bytes 2752520 | tf_op jit(solution)/shard_map/ppermute | solution.py:131
  73.0 19.7 %collective-permute-start.16 = (f32[32,56,128]{2,1,0:T(8,128)S(1)}, f32[32,56,128]{2,1,0:T(8,128)}, u32[]{:S(2)}, u32[]{:S(2)}) collective-permute-start(f32[32,56,128]{2,1,0:T(8,128)S(1)} %get-tuple-element.15), channel_id=1, source_target_pairs={{0,16},{8,56},{1,17},{9,57},{2,18},{10,58},{3,19},{11,59},{4,20},{... | collective-permute-start | bytes 2752520 | tf_op jit(solution)/shard_map/ppermute | solution.py:131
  73.3 19.3 %collective-permute-start.3 = (f32[32,56,128]{2,1,0:T(8,128)S(1)}, f32[32,56,128]{2,1,0:T(8,128)}, u32[]{:S(2)}, u32[]{:S(2)}) collective-permute-start(f32[32,56,128]{2,1,0:T(8,128)S(1)} %get-tuple-element.16), channel_id=1, source_target_pairs={{0,64},{8,200},{1,65},{9,201},{2,66},{10,202},{3,67},{11,203},{4,6... | collective-permute-start | bytes 2752520 | tf_op jit(solution)/shard_map/ppermute | solution.py:131
  73.6 8.8 %collective-permute-start.24 = (f32[16,56,128]{2,1,0:T(8,128)}, f32[16,56,128]{2,1,0:T(8,128)}, u32[]{:S(2)}, u32[]{:S(2)}) collective-permute-start(f32[16,56,128]{2,1,0:T(8,128)} %get-tuple-element.18), channel_id=1, source_target_pairs={{0,1},{8,15},{1,2},{9,8},{2,3},{10,9},{3,4},{11,10},{4,5},{12,11},... | collective-permute-start | bytes 1376264 | tf_op jit(solution)/shard_map/ppermute | solution.py:131
  84.1 32.5 %collective-permute-start.28 = (f32[16,56,128]{2,1,0:T(8,128)S(1)}, f32[16,56,128]{2,1,0:T(8,128)S(1)}, u32[]{:S(2)}, u32[]{:S(2)}) collective-permute-start(f32[16,56,128]{2,1,0:T(8,128)S(1)} %get-tuple-element.23), channel_id=1, source_target_pairs={{0,7},{8,9},{1,0},{9,10},{2,1},{10,11},{3,2},{11,12},{4,3},{12,13}... | collective-permute-start | bytes 1376264 | tf_op jit(solution)/shard_map/ppermute | solution.py:131
  92.1 26.9 %collective-permute-start.25 = (f32[16,56,128]{2,1,0:T(8,128)S(1)}, f32[16,56,128]{2,1,0:T(8,128)S(1)}, u32[]{:S(2)}, u32[]{:S(2)}) collective-permute-start(f32[16,56,128]{2,1,0:T(8,128)S(1)} %get-tuple-element.24), channel_id=1, source_target_pairs={{0,1},{8,15},{1,2},{9,8},{2,3},{10,9},{3,4},{11,10},{4,5},{12,11},... | collective-permute-start | bytes 1376264 | tf_op jit(solution)/shard_map/ppermute | solution.py:131
  95.8 12.7 %collective-permute-start.6 = (f32[8,56,128]{2,1,0:T(8,128)S(1)}, f32[8,56,128]{2,1,0:T(8,128)S(1)}, u32[]{:S(2)}, u32[]{:S(2)}) collective-permute-start(f32[8,56,128]{2,1,0:T(8,128)S(1)} %get-tuple-element.29), channel_id=1, source_target_pairs={{0,16},{8,56},{1,17},{9,57},{2,18},{10,58},{3,19},{11,59},{4,20},{... | collective-permute-start | bytes 688136 | tf_op jit(solution)/shard_map/ppermute | solution.py:131
  96.7 15.5 %collective-permute-start.8 = (f32[8,56,128]{2,1,0:T(8,128)S(1)}, f32[8,56,128]{2,1,0:T(8,128)S(1)}, u32[]{:S(2)}, u32[]{:S(2)}) collective-permute-start(f32[8,56,128]{2,1,0:T(8,128)S(1)} %get-tuple-element.30), channel_id=1, source_target_pairs={{0,32},{8,40},{1,33},{9,41},{2,34},{10,42},{3,35},{11,43},{4,36},{... | collective-permute-start | bytes 688136 | tf_op jit(solution)/shard_map/ppermute | solution.py:131
  100.1 14.5 %collective-permute-start.7 = (f32[8,56,128]{2,1,0:T(8,128)S(1)}, f32[8,56,128]{2,1,0:T(8,128)S(1)}, u32[]{:S(2)}, u32[]{:S(2)}) collective-permute-start(f32[8,56,128]{2,1,0:T(8,128)S(1)} %get-tuple-element.31), channel_id=1, source_target_pairs={{0,48},{8,24},{1,49},{9,25},{2,50},{10,26},{3,51},{11,27},{4,52},{... | collective-permute-start | bytes 688136 | tf_op jit(solution)/shard_map/ppermute | solution.py:131
  108.5 22.5 %collective-permute-start.18 = (f32[4,2,56,128]{3,2,1,0:T(8,128)S(1)}, f32[4,2,56,128]{3,2,1,0:T(8,128)S(1)}, u32[]{:S(2)}, u32[]{:S(2)}) collective-permute-start(f32[4,2,56,128]{3,2,1,0:T(8,128)S(1)} %pad_maximum_fusion), channel_id=1, source_target_pairs={{0,6},{8,10},{1,7},{9,11},{2,0},{10,12},{3,1},{11,13},{4,2},{12,14... | collective-permute-start | bytes 688136 | tf_op jit(solution)/shard_map/ppermute | solution.py:131
  112.2 19.4 %collective-permute-start.19 = (f32[4,2,56,128]{3,2,1,0:T(8,128)S(1)}, f32[4,2,56,128]{3,2,1,0:T(8,128)S(1)}, u32[]{:S(2)}, u32[]{:S(2)}) collective-permute-start(f32[4,2,56,128]{3,2,1,0:T(8,128)S(1)} %pad_maximum_fusion.1), channel_id=1, source_target_pairs={{0,2},{8,14},{1,3},{9,15},{2,4},{10,8},{3,5},{11,9},{4,6},{12,10},... | collective-permute-start | bytes 688136 | tf_op jit(solution)/shard_map/ppermute | solution.py:131
  116.6 12.3 %collective-permute-start.10 = (f32[2,56,128]{2,1,0:T(8,128)S(1)}, f32[2,56,128]{2,1,0:T(8,128)S(1)}, u32[]{:S(2)}, u32[]{:S(2)}) collective-permute-start(f32[2,56,128]{2,1,0:T(8,128)S(1)} %pad_maximum_fusion.3), channel_id=1, source_target_pairs={{0,2},{8,14},{1,3},{9,15},{2,4},{10,8},{3,5},{11,9},{4,6},{12,10},... | collective-permute-start | bytes 172040 | tf_op jit(solution)/shard_map/ppermute | solution.py:131
  120.6 22.0 %collective-permute-start.29 = (f32[16,56,128]{2,1,0:T(8,128)S(1)}, f32[16,56,128]{2,1,0:T(8,128)S(1)}, u32[]{:S(2)}, u32[]{:S(2)}) collective-permute-start(f32[16,56,128]{2,1,0:T(8,128)S(1)} %get-tuple-element.21), channel_id=1, source_target_pairs={{0,7},{8,9},{1,0},{9,10},{2,1},{10,11},{3,2},{11,12},{4,3},{12,13}... | collective-permute-start | bytes 1376264 | tf_op jit(solution)/shard_map/ppermute | solution.py:131
  121.9 22.3 %collective-permute-start.26 = (f32[16,56,128]{2,1,0:T(8,128)S(1)}, f32[16,56,128]{2,1,0:T(8,128)S(1)}, u32[]{:S(2)}, u32[]{:S(2)}) collective-permute-start(f32[16,56,128]{2,1,0:T(8,128)S(1)} %get-tuple-element.22), channel_id=1, source_target_pairs={{0,1},{8,15},{1,2},{9,8},{2,3},{10,9},{3,4},{11,10},{4,5},{12,11},... | collective-permute-start | bytes 1376264 | tf_op jit(solution)/shard_map/ppermute | solution.py:131
  128.9 7.6 %collective-permute-start.11 = (f32[1,56,128]{2,1,0:T(8,128)S(1)}, f32[1,56,128]{2,1,0:T(8,128)S(1)}, u32[]{:S(2)}, u32[]{:S(2)}) collective-permute-start(f32[1,56,128]{2,1,0:T(8,128)S(1)} %get-tuple-element.40), channel_id=1, source_target_pairs={{0,2},{8,14},{1,3},{9,15},{2,4},{10,8},{3,5},{11,9},{4,6},{12,10},... | collective-permute-start | bytes 86024 | tf_op jit(solution)/shard_map/ppermute | solution.py:131
  131.0 8.3 %collective-permute-start.12 = (f32[1,56,128]{2,1,0:T(8,128)S(1)}, f32[1,56,128]{2,1,0:T(8,128)S(1)}, u32[]{:S(2)}, u32[]{:S(2)}) collective-permute-start(f32[1,56,128]{2,1,0:T(8,128)S(1)} %get-tuple-element.41), channel_id=1, source_target_pairs={{0,1},{8,15},{1,2},{9,8},{2,3},{10,9},{3,4},{11,10},{4,5},{12,11},... | collective-permute-start | bytes 86024 | tf_op jit(solution)/shard_map/ppermute | solution.py:131
  131.6 11.0 %collective-permute-start.13 = (f32[1,56,128]{2,1,0:T(8,128)S(1)}, f32[1,56,128]{2,1,0:T(8,128)S(1)}, u32[]{:S(2)}, u32[]{:S(2)}) collective-permute-start(f32[1,56,128]{2,1,0:T(8,128)S(1)} %get-tuple-element.42), channel_id=1, source_target_pairs={{0,7},{8,9},{1,0},{9,10},{2,1},{10,11},{3,2},{11,12},{4,3},{12,13}... | collective-permute-start | bytes 86024 | tf_op jit(solution)/shard_map/ppermute | solution.py:131
  136.5 9.0 %collective-permute-start.20 = (f32[4,1,56,128]{3,2,1,0:T(8,128)S(1)}, f32[4,1,56,128]{3,2,1,0:T(8,128)S(1)}, u32[]{:S(2)}, u32[]{:S(2)}) collective-permute-start(f32[4,1,56,128]{3,2,1,0:T(8,128)S(1)} %get-tuple-element.27), channel_id=1, source_target_pairs={{0,2},{8,14},{1,3},{9,15},{2,4},{10,8},{3,5},{11,9},{4,6},{12,10},... | collective-permute-start | bytes 344072 | tf_op jit(solution)/shard_map/ppermute | solution.py:131
  139.3 9.1 %collective-permute-start.21 = (f32[4,1,56,128]{3,2,1,0:T(8,128)S(1)}, f32[4,1,56,128]{3,2,1,0:T(8,128)S(1)}, u32[]{:S(2)}, u32[]{:S(2)}) collective-permute-start(f32[4,1,56,128]{3,2,1,0:T(8,128)S(1)} %get-tuple-element.28), channel_id=1, source_target_pairs={{0,1},{8,15},{1,2},{9,8},{2,3},{10,9},{3,4},{11,10},{4,5},{12,11},... | collective-permute-start | bytes 344072 | tf_op jit(solution)/shard_map/ppermute | solution.py:131
  142.6 16.1 %collective-permute-start.14 = (f32[56,128]{1,0:T(8,128)S(1)}, f32[56,128]{1,0:T(8,128)S(1)}, u32[]{:S(2)}, u32[]{:S(2)}) collective-permute-start(f32[56,128]{1,0:T(8,128)S(1)} %fusion.24), channel_id=1, source_target_pairs={{0,128},{8,136},{1,129},{9,137},{2,130},{10,138},{3,131},{11,139},... | collective-permute-start | bytes 86024 | tf_op jit(solution)/shard_map/ppermute | solution.py:131
  145.4 9.5 %collective-permute-start.30 = (f32[4,56,128]{2,1,0:T(8,128)S(1)}, f32[4,56,128]{2,1,0:T(8,128)S(1)}, u32[]{:S(2)}, u32[]{:S(2)}) collective-permute-start(f32[4,56,128]{2,1,0:T(8,128)S(1)} %get-tuple-element.37), channel_id=1, source_target_pairs={{0,16},{8,56},{1,17},{9,57},{2,18},{10,58},{3,19},{11,59},{4,20},{... | collective-permute-start | bytes 344072 | tf_op jit(solution)/shard_map/ppermute | solution.py:131
  145.5 9.4 %collective-permute-start.32 = (f32[4,56,128]{2,1,0:T(8,128)S(1)}, f32[4,56,128]{2,1,0:T(8,128)S(1)}, u32[]{:S(2)}, u32[]{:S(2)}) collective-permute-start(f32[4,56,128]{2,1,0:T(8,128)S(1)} %get-tuple-element.38), channel_id=1, source_target_pairs={{0,32},{8,40},{1,33},{9,41},{2,34},{10,42},{3,35},{11,43},{4,36},{... | collective-permute-start | bytes 344072 | tf_op jit(solution)/shard_map/ppermute | solution.py:131
  155.1 9.5 %collective-permute-start.35 = (f32[2,2,56,128]{3,2,1,0:T(8,128)S(1)}, f32[2,2,56,128]{3,2,1,0:T(8,128)S(1)}, u32[]{:S(2)}, u32[]{:S(2)}) collective-permute-start(f32[2,2,56,128]{3,2,1,0:T(8,128)S(1)} %get-tuple-element.48), channel_id=1, source_target_pairs={{0,192},{8,72},{1,193},{9,73},{2,194},{10,74},{3,195},{11,75},{4,1... | collective-permute-start | bytes 344072 | tf_op jit(solution)/shard_map/ppermute | solution.py:131
  156.5 8.5 %collective-permute-start.34 = (f32[2,2,56,128]{3,2,1,0:T(8,128)S(1)}, f32[2,2,56,128]{3,2,1,0:T(8,128)S(1)}, u32[]{:S(2)}, u32[]{:S(2)}) collective-permute-start(f32[2,2,56,128]{3,2,1,0:T(8,128)S(1)} %get-tuple-element.48), channel_id=1, source_target_pairs={{0,64},{8,200},{1,65},{9,201},{2,66},{10,202},{3,67},{11,203},{4,6... | collective-permute-start | bytes 344072 | tf_op jit(solution)/shard_map/ppermute | solution.py:131
  (5 other events, 28.9 us)

commit v2 on v0

v2 whole, which is shorter than its diff:
```python
import jax
import jax.numpy as jnp
from jax import lax
from jax.experimental import pallas as pl
from jax.experimental.pallas import tpu as pltpu
from jax.sharding import PartitionSpec as P

AXES = ("dcn", "gx", "gy")
STEP = 768
RX, RY = 8, 8
RZ = 21 - RX - RY
CX, CY, CZ = 32 * RX, 32 * RY, 16 * RZ
ORDER = (("x", 2), ("y", 2), ("z", 4), None, ("z", 5), ("z", 3), ("x", 3), ("y", 3), ("x", 1), ("y", 1),
         ("z", 6), ("z", 2), ("z", 7), ("z", 1), ("x", 0), ("y", 0), ("z", 0))
SIZE = {"x": CX, "y": CY, "z": CZ}


def layout():
    at, row, cut = {}, 0, 0
    for item in ORDER:
        if item is None:
            cut = row
        else:
            at[item] = row
            row += SIZE[item[0]]
    return at, cut, row


AT, CUT, ROWS = layout()


def pick(axis, k, n):
    value = jnp.int32(AT[axis, 0])
    for i in range(1, n):
        value = jnp.where(k == i, jnp.int32(AT[axis, i]), value)
    return value


def grad_kernel(where_ref, h_ref, c_ref, keep, send1, send2, h_buf, c_buf, acc, h_sem, c_sem, sem):
    x, y, z, core = where_ref[0], where_ref[1], where_ref[2], where_ref[3]
    steps = h_ref.shape[1] // STEP
    fetch_c = pltpu.make_async_copy(c_ref, c_buf, c_sem)
    fetch_h = [
        pltpu.make_async_copy(h_ref.at[:, pl.ds(i * STEP, STEP)], h_buf.at[i], h_sem.at[i])
        for i in range(steps)
    ]
    fetch_h[0].start()
    fetch_c.start()
    for i in range(1, steps):
        fetch_h[i].start()
    fetch_c.wait()
    flat = acc.reshape(5376 * 8, 128)
    parts = acc.reshape(16, 8, 2, 21, 8, 128)

    def copy_out(src, row, mine):
        count = 1
        for n in src.shape[:-2]:
            count *= n

        def put(dst, base):
            to = dst.at[pl.ds(row - base, count)].reshape(src.shape)
            pltpu.make_async_copy(src, to, sem).start()

        pl.when(mine)(lambda: put(keep, 0))
        pl.when(jnp.logical_not(mine) & (row < CUT))(lambda: put(send1, 0))
        pl.when(jnp.logical_not(mine) & (row >= CUT))(lambda: put(send2, CUT))

    def block_out(b):
        c2, y2, xl = b % 2, b // 2 % 4, b // 8
        sign = 1 - 2 * c2
        mine = core == c2
        rely = lax.rem(sign * (y2 - y) + 4, 4)
        for xh in range(2):
            relx = lax.rem(sign * (2 * xh + xl - x) + 4, 4)
            to_x = pick("x", relx, 4) + rely * (8 * RX)
            to_y = pick("y", rely, 4) + relx * (8 * RY)
            copy_out(parts.at[b, :, xh, pl.ds(0, RX)], to_x, mine)
            copy_out(parts.at[b, :, xh, pl.ds(RX, RY)], to_y, mine)
        for z2 in range(8):
            relz = lax.rem(sign * (z2 - z) + 8, 8)
            copy_out(
                parts.at[b, z2, :, pl.ds(RX + RY, RZ)],
                pick("z", relz, 8) + (rely * 4 + xl * 2) * RZ,
                mine,
            )

    out = 0
    for i in range(steps):
        fetch_h[i].wait()
        for j in range(0, STEP, 256):
            prod = lax.dot_general(
                h_buf[i, :, j : j + 256],
                c_buf[...],
                (((0,), (0,)), ((), ())),
                preferred_element_type=jnp.float32,
            )
            for s in range(8):
                flat[pl.ds((i * STEP + j) * 8 + s, 256, stride=8), :] = prod[:, s * 128 : (s + 1) * 128]
        while (out + 1) * 336 <= (i + 1) * STEP:
            block_out(out)
            out += 1
    for ref in (keep, send1, send2):
        pltpu.make_async_copy(ref, ref, sem).wait()


def local_grad(where, hidden_in, key_cotangent):
    tokens, width = hidden_in.shape
    keys = key_cotangent.shape[1]
    shape = lambda n: jax.ShapeDtypeStruct((n, 8, 128), jnp.float32)
    anywhere = pl.BlockSpec(memory_space=pl.ANY)
    return pl.pallas_call(
        grad_kernel,
        out_shape=(shape(ROWS), shape(CUT), shape(ROWS - CUT)),
        in_specs=[pl.BlockSpec(memory_space=pltpu.SMEM), anywhere, anywhere],
        out_specs=(anywhere,) * 3,
        scratch_shapes=[
            pltpu.VMEM((width // STEP, tokens, STEP), jnp.bfloat16),
            pltpu.VMEM((tokens, keys), jnp.bfloat16),
            pltpu.VMEM((width, 8, 128), jnp.float32),
            pltpu.SemaphoreType.DMA((width // STEP,)),
            pltpu.SemaphoreType.DMA,
            pltpu.SemaphoreType.DMA,
        ],
        compiler_params=pltpu.CompilerParams(vmem_limit_bytes=60 * 1024 * 1024),
        cost_estimate=pl.CostEstimate(
            flops=2 * tokens * width * keys,
            bytes_accessed=2 * tokens * (width + keys) + 4 * width * keys,
            transcendentals=0,
        ),
        name="local_grad",
    )(where, hidden_in, key_cotangent)


def place(x, y, z, c):
    return (x // 2) * 128 + (((x % 2) * 4 + y) * 2 + c) * 8 + z


EVERY = [(x, y, z, c) for x in range(4) for y in range(4) for z in range(8) for c in range(2)]
SWAP = [(place(x, y, z, c), place(x, y, z, 1 - c)) for x, y, z, c in EVERY]
PAIR_X = [(place(x, y, z, c), place(x ^ 1, y, z, c)) for x, y, z, c in EVERY]


def moves(axis, hop):
    pairs = []
    for x, y, z, c in EVERY:
        at = [x, y, z]
        at[axis] = (at[axis] + (hop if c == 0 else -hop)) % (4, 4, 8)[axis]
        pairs.append((place(x, y, z, c), place(*at, c)))
    return pairs


def send(a, pairs):
    return lax.ppermute(a, AXES, pairs)


def go(a, axis, hop):
    return send(a, moves(axis, hop))


def after(value, token):
    anywhere = pl.BlockSpec(memory_space=pl.ANY)
    return pl.pallas_call(
        lambda *refs: None,
        out_shape=jax.ShapeDtypeStruct(value.shape, value.dtype),
        in_specs=[anywhere, pl.BlockSpec(memory_space=pltpu.SMEM)],
        out_specs=anywhere,
        input_output_aliases={0: 0},
        cost_estimate=pl.CostEstimate(flops=0, bytes_accessed=0, transcendentals=0),
        name="after",
    )(value, token.reshape(1))


def zero(a):
    return jnp.sum(a[:1]) * jnp.float32(0)


def body(hidden_in, key_cotangent):
    count_all = (
        hidden_in.shape[0] * lax.axis_size("dcn") * lax.axis_size("gx") * lax.axis_size("gy")
    )
    factor = jnp.float32(1.0 / count_all**0.5)
    dcn, gx, z = (lax.axis_index(a) for a in AXES)
    core, y, xl = lax.rem(gx, 2), lax.rem(lax.div(gx, 2), 4), lax.div(gx, 8)
    x = dcn * 2 + xl
    sign = 1 - 2 * core
    where = jnp.stack([x, y, z, core]).astype(jnp.int32)
    keep, send1, send2 = local_grad(where, hidden_in, key_cotangent)

    got1 = send(send1, SWAP)
    got2 = send(after(send2, zero(got1)), SWAP)

    def own(name, k):
        row, count = AT[name, k], SIZE[name]
        got, base = (got1, 0) if row < CUT else (got2, CUT)
        return keep[row : row + count] + got[row - base : row - base + count]

    def ring4(name, axis):
        a = go(own(name, 2), axis, 1)
        b = go(own(name, 3), axis, -1)
        a = go(a + own(name, 1), axis, 1)
        return a + b + own(name, 0)

    def ring8(name, axis):
        a = go(own(name, 4), axis, 1)
        b = go(own(name, 5), axis, -1)
        a = go(a + own(name, 3), axis, 1)
        b = go(b + own(name, 6), axis, -1)
        a = go(a + own(name, 2), axis, 1)
        b = go(b + own(name, 7), axis, -1)
        a = go(a + own(name, 1), axis, 1)
        return a + b + own(name, 0)

    part_z = ring8("z", 2)
    part_x = ring4("x", 0)
    part_y = ring4("y", 1)

    def direct(part, axis):
        n = part.shape[0] // 4
        a = go(part[2 * n : 3 * n], axis, 1)
        b = go(part[3 * n :], axis, -1)
        a = go(a + part[n : 2 * n], axis, 1)
        return a + b + part[:n]

    part_xz = jnp.concatenate(
        [part_x.reshape(4, 8 * RX, 8, 128), part_z.reshape(4, 4 * RZ, 8, 128)], axis=1
    )
    part_xz = direct(part_xz.reshape(-1, 8, 128), 1)
    part_x, part_z = part_xz[: 8 * RX], part_xz[8 * RX :].reshape(2, 2 * RZ, 8, 128)
    part_y = direct(part_y, 0)

    both = jnp.concatenate(
        [part_x.reshape(8, RX, 8, 128), part_y.reshape(8, RY, 8, 128)], axis=1
    )

    def at(k):
        return lax.dynamic_index_in_dim(both, lax.rem(z + sign * k + 16, 8), keepdims=False)

    up = go(jnp.concatenate([at(4), at(3)]), 2, 2)
    down = go(jnp.concatenate([at(-3), at(-2)]), 2, -2)
    n = RX + RY
    a2 = go(up[:n] + at(2), 2, 2)
    a1 = go(up[n:] + at(1), 2, 1)
    b1 = go(down[:n] + at(-1), 2, -1)
    both = at(0) + down[n:] + a2 + a1 + b1
    part_z = lax.dynamic_index_in_dim(part_z, xl, keepdims=False) + send(
        lax.dynamic_index_in_dim(part_z, 1 - xl, keepdims=False), PAIR_X
    )

    mine = jnp.concatenate([both, part_z])
    theirs = go(mine, 0, 2)
    part_z = (part_z + theirs[n:]).reshape(2, RZ, 8, 128)
    first, second = jnp.where(dcn == 0, both, theirs[:n]), jnp.where(dcn == 0, theirs[:n], both)
    result = jnp.concatenate([first, part_z[0], second, part_z[1]])
    return result.reshape(-1, 1024) * factor


def solution(mesh):
    placed = (P(AXES, None), P(AXES, None))
    return jax.shard_map(
        body, mesh=mesh, in_specs=placed, out_specs=P(("gx", "gy"), None), check_vma=False
    )
```

time: 264 us -> 138 us (0.52)
  waiting for transfers between devices: 191 us -> 55.5 us
  starting transfers between devices: 4.98 us -> 42.1 us
  blocking collectives: 24.3 us -> 0 us
  matrix products: 24.2 us -> 0 us
  Pallas kernels: 0 us -> 21.4 us
  other arithmetic: 1.63 us -> 17.7 us
  between operations: 13.8 us -> 0.74 us
  local copies, waits for them, and re-layouts: 3.85 us -> 0.1 us
    reduce_scatter x2 -> x0, waiting for transfers between devices: 154 us -> none  [body(): lax.psum_scatter(jnp.einsum('tr,tc->rc', hidden_in, cotangent, preferred_...]
    ppermute x0 -> x28, waiting for transfers between devices: none -> 55.5 us  [send(): return lax.ppermute(a, AXES, pairs)]
    ppermute x0 -> x28, starting transfers between devices: none -> 42.1 us  [send(): return lax.ppermute(a, AXES, pairs)]
    psum x1 -> x0, waiting for transfers between devices: 33.3 us -> none  [body(): pieces.append(lax.psum(owned, 'dcn'))]
    unnamed x1 -> x0, blocking collectives: 24.3 us -> none
    dot_general x2 -> x0, matrix products: 24.2 us -> none  [body(): jnp.einsum('tr,tc->rc', hidden_in, cotangent, preferred_element_type=jnp....]
    pallas_call x0 -> x2, Pallas kernels: none -> 21.4 us  [the longest x1 21.4 us: local_grad(): pl.pallas_call(grad_kernel, out_shape=(shape(ROWS), shape(CUT), shape(ROW...]
    add x0 -> x15, other arithmetic: none -> 14.1 us  [the longest x4 6.58 us: own(): return keep[row:row + count] + got[row - base:row - base + count]]
  transfers between devices with their start and end apart: 5 -> 28, of which waited for: 5 -> 18; matrix products, arithmetic and copies ran while one was open for 5% -> 11% of each run, Pallas kernels for 0% -> 0%
where the time goes in v2:
time: 138 us; the launch traced here: 137 us
  waiting for transfers between devices  55.5 us (40%)
  starting transfers between devices  42.1 us (31%)
  Pallas kernels  21.4 us (16%)
  other arithmetic  17.7 us (13%)
    ppermute x28, waiting for transfers between devices, send(): return lax.ppermute(a, AXES, pairs)  55.5 us
    ppermute x28, starting transfers between devices, send(): return lax.ppermute(a, AXES, pairs)  42.1 us
    pallas_call x1, Pallas kernels, local_grad(): pl.pallas_call(grad_kernel, out_shape=(shape(ROWS), shape(CUT), shape(ROW...  21.4 us
    add x4, other arithmetic, own(): return keep[row:row + count] + got[row - base:row - base + count]  6.58 us
  transfers between devices with their start and end apart: 28, of which 18 were waited for; matrix products, arithmetic and copies ran while one was open for 11% of the time, Pallas kernels for 0%

profile of v2, /device:TPU:32, one launch (start us, length us, event | category | flops | bytes accessed | tf_op | source)
XLA Modules:
  0.0 137.5 jit_solution(4029531607263627443)
XLA Ops:
  0.6 21.4 %local_grad.1 = (f32[2688,8,128]{2,1,0:T(8,128)}, f32[592,8,128]{2,1,0:T(8,128)}, f32[2096,8,128]{2,1,0:T(8,128)}) custom-call(s32[4]{0:T(128)} %pad_add_fusion.where_ref, bf16[1024,5376]{1,0:T(8,128)(2,1)} %h_ref.1, bf16[1024,1024]{1,0:T(8,128)(2,1)} %c_ref.1), custom_call_target="tpu_custom_call" | custom-call | flops 11274289152 | bytes 35127296 | tf_op jit(solution)/shard_map/local_grad/pallas_call | solution.py:111
  22.1 4.8 %collective-permute-done = f32[592,8,128]{2,1,0:T(8,128)S(1)} collective-permute-done((f32[592,8,128]{2,1,0:T(8,128)}, f32[592,8,128]{2,1,0:T(8,128)S(1)}, u32[]{:S(2)}, u32[]{:S(2)}) %collective-permute-start) | collective-permute-done | bytes 2424864 | tf_op jit(solution)/shard_map/ppermute | solution.py:153
  28.3 1.8 %slice_add_fusion.3 = (f32[256,8,128]{2,1,0:T(8,128)S(1)}, f32[256,8,128]{2,1,0:T(8,128)S(1)}) fusion(f32[592,8,128]{2,1,0:T(8,128)S(1)} %collective-permute-done, f32[2688,8,128]{2,1,0:T(8,128)} %get-tuple-element.8), kind=kLoop, calls=%fused_computation.27 | loop fusion | flops 524288 | bytes 6291456 | tf_op jit(solution)/shard_map/add | solution.py:195
  30.1 1.7 %collective-permute-start.15 = (f32[256,8,128]{2,1,0:T(8,128)S(1)}, f32[256,8,128]{2,1,0:T(8,128)S(1)}, u32[]{:S(2)}, u32[]{:S(2)}) collective-permute-start(f32[256,8,128]{2,1,0:T(8,128)S(1)} %get-tuple-element.23), channel_id=1, source_target_pairs={{0,16},{8,56},{1,17},{9,57},{2,18},{10,58},{3,19},{11,59},{4,20},{... | collective-permute-start | bytes 3145736 | tf_op jit(solution)/shard_map/ppermute | solution.py:153
  31.8 1.5 %collective-permute-start.1 = (f32[256,8,128]{2,1,0:T(8,128)S(1)}, f32[256,8,128]{2,1,0:T(8,128)S(1)}, u32[]{:S(2)}, u32[]{:S(2)}) collective-permute-start(f32[256,8,128]{2,1,0:T(8,128)S(1)} %get-tuple-element.24), channel_id=1, source_target_pairs={{0,64},{8,200},{1,65},{9,201},{2,66},{10,202},{3,67},{11,203},{4,6... | collective-permute-start | bytes 3145736 | tf_op jit(solution)/shard_map/ppermute | solution.py:153
  34.3 2.0 %collective-permute-start.5 = (f32[80,8,128]{2,1,0:T(8,128)S(1)}, f32[80,8,128]{2,1,0:T(8,128)S(1)}, u32[]{:S(2)}, u32[]{:S(2)}) collective-permute-start(f32[80,8,128]{2,1,0:T(8,128)S(1)} %slice_add_fusion.15), channel_id=1, source_target_pairs={{0,1},{8,15},{1,2},{9,8},{2,3},{10,9},{3,4},{11,10},{4,5},{12,11},... | collective-permute-start | bytes 983048 | tf_op jit(solution)/shard_map/ppermute | solution.py:153
  36.3 5.2 %collective-permute-done.5 = f32[80,8,128]{2,1,0:T(8,128)S(1)} collective-permute-done((f32[80,8,128]{2,1,0:T(8,128)S(1)}, f32[80,8,128]{2,1,0:T(8,128)S(1)}, u32[]{:S(2)}, u32[]{:S(2)}) %collective-permute-start.5) | collective-permute-done | bytes 327712 | tf_op jit(solution)/shard_map/ppermute | solution.py:153
  43.0 3.6 %collective-permute-start.9 = (f32[80,8,128]{2,1,0:T(8,128)S(1)}, f32[80,8,128]{2,1,0:T(8,128)S(1)}, u32[]{:S(2)}, u32[]{:S(2)}) collective-permute-start(f32[80,8,128]{2,1,0:T(8,128)S(1)} %get-tuple-element.21), channel_id=1, source_target_pairs={{0,7},{8,9},{1,0},{9,10},{2,1},{10,11},{3,2},{11,12},{4,3},{12,13}... | collective-permute-start | bytes 983048 | tf_op jit(solution)/shard_map/ppermute | solution.py:153
  47.8 2.7 %slice_add_fusion.1 = (f32[256,8,128]{2,1,0:T(8,128)S(1)}, f32[256,8,128]{2,1,0:T(8,128)S(1)}, f32[256,8,128]{2,1,0:T(8,128)S(1)}, f32[256,8,128]{2,1,0:T(8,128)S(1)}) fusion(f32[2096,8,128]{2,1,0:T(8,128)S(1)} %collective-permute-done.2, f32[2688,8,128]{2,1,0:T(8,128)} %get-tuple-element.8, f32[256,8,128]{2,1,0:T(8,128)S(1)} %collective-permute-done.15, ...), kind=kLoop, calls=%fused_computation.24 | loop fusion | flops 1572864 | bytes 14680064 | tf_op jit(solution)/shard_map/add | solution.py:195
  50.5 1.6 %collective-permute-start.16 = (f32[256,8,128]{2,1,0:T(8,128)S(1)}, f32[256,8,128]{2,1,0:T(8,128)S(1)}, u32[]{:S(2)}, u32[]{:S(2)}) collective-permute-start(f32[256,8,128]{2,1,0:T(8,128)S(1)} %get-tuple-element.14), channel_id=1, source_target_pairs={{0,16},{8,56},{1,17},{9,57},{2,18},{10,58},{3,19},{11,59},{4,20},{... | collective-permute-start | bytes 3145736 | tf_op jit(solution)/shard_map/ppermute | solution.py:153
  52.1 1.7 %collective-permute-start.17 = (f32[256,8,128]{2,1,0:T(8,128)S(1)}, f32[256,8,128]{2,1,0:T(8,128)S(1)}, u32[]{:S(2)}, u32[]{:S(2)}) collective-permute-start(f32[256,8,128]{2,1,0:T(8,128)S(1)} %get-tuple-element.13), channel_id=1, source_target_pairs={{0,48},{8,24},{1,49},{9,25},{2,50},{10,26},{3,51},{11,27},{4,52},{... | collective-permute-start | bytes 3145736 | tf_op jit(solution)/shard_map/ppermute | solution.py:153
  54.4 2.6 %collective-permute-start.4 = (f32[256,8,128]{2,1,0:T(8,128)S(1)}, f32[256,8,128]{2,1,0:T(8,128)S(1)}, u32[]{:S(2)}, u32[]{:S(2)}) collective-permute-start(f32[256,8,128]{2,1,0:T(8,128)S(1)} %get-tuple-element.15), channel_id=1, source_target_pairs={{0,192},{8,72},{1,193},{9,73},{2,194},{10,74},{3,195},{11,75},{4,1... | collective-permute-start | bytes 3145736 | tf_op jit(solution)/shard_map/ppermute | solution.py:153
  58.2 2.6 %collective-permute-start.10 = (f32[80,8,128]{2,1,0:T(8,128)S(1)}, f32[80,8,128]{2,1,0:T(8,128)S(1)}, u32[]{:S(2)}, u32[]{:S(2)}) collective-permute-start(f32[80,8,128]{2,1,0:T(8,128)S(1)} %get-tuple-element.19), channel_id=1, source_target_pairs={{0,7},{8,9},{1,0},{9,10},{2,1},{10,11},{3,2},{11,12},{4,3},{12,13}... | collective-permute-start | bytes 983048 | tf_op jit(solution)/shard_map/ppermute | solution.py:153
  60.8 4.6 %collective-permute-done.10 = f32[80,8,128]{2,1,0:T(8,128)S(1)} collective-permute-done((f32[80,8,128]{2,1,0:T(8,128)S(1)}, f32[80,8,128]{2,1,0:T(8,128)S(1)}, u32[]{:S(2)}, u32[]{:S(2)}) %collective-permute-start.10) | collective-permute-done | bytes 327712 | tf_op jit(solution)/shard_map/ppermute | solution.py:153
  65.4 1.9 %collective-permute-start.7 = (f32[80,8,128]{2,1,0:T(8,128)S(1)}, f32[80,8,128]{2,1,0:T(8,128)S(1)}, u32[]{:S(2)}, u32[]{:S(2)}) collective-permute-start(f32[80,8,128]{2,1,0:T(8,128)S(1)} %get-tuple-element.20), channel_id=1, source_target_pairs={{0,1},{8,15},{1,2},{9,8},{2,3},{10,9},{3,4},{11,10},{4,5},{12,11},... | collective-permute-start | bytes 983048 | tf_op jit(solution)/shard_map/ppermute | solution.py:153
  67.2 7.0 %collective-permute-done.7 = f32[80,8,128]{2,1,0:T(8,128)S(1)} collective-permute-done((f32[80,8,128]{2,1,0:T(8,128)S(1)}, f32[80,8,128]{2,1,0:T(8,128)S(1)}, u32[]{:S(2)}, u32[]{:S(2)}) %collective-permute-start.7) | collective-permute-done | bytes 327712 | tf_op jit(solution)/shard_map/ppermute | solution.py:153
  77.5 2.1 %collective-permute-start.11 = (f32[80,8,128]{2,1,0:T(8,128)S(1)}, f32[80,8,128]{2,1,0:T(8,128)S(1)}, u32[]{:S(2)}, u32[]{:S(2)}) collective-permute-start(f32[80,8,128]{2,1,0:T(8,128)S(1)} %get-tuple-element.17), channel_id=1, source_target_pairs={{0,7},{8,9},{1,0},{9,10},{2,1},{10,11},{3,2},{11,12},{4,3},{12,13}... | collective-permute-start | bytes 983048 | tf_op jit(solution)/shard_map/ppermute | solution.py:153
  80.9 2.2 %fusion = (f32[256,8,128]{2,1,0:T(8,128)S(1)}, f32[256,8,128]{2,1,0:T(8,128)S(1)}) fusion(f32[2096,8,128]{2,1,0:T(8,128)S(1)} %collective-permute-done.2, f32[2688,8,128]{2,1,0:T(8,128)} %get-tuple-element.8, f32[256,8,128]{2,1,0:T(8,128)S(1)} %collective-permute-done.16, f32[256,8,128]{2,1,0:T(8,128)S(1)} %collective-permute-done.17, ...), kind=kLoop, calls=%fused_computation.23 | loop fusion | flops 1572864 | bytes 10485760 | tf_op jit(solution)/shard_map/add | solution.py:201
  83.1 3.8 %collective-permute-done.8 = f32[80,8,128]{2,1,0:T(8,128)S(1)} collective-permute-done((f32[80,8,128]{2,1,0:T(8,128)S(1)}, f32[80,8,128]{2,1,0:T(8,128)S(1)}, u32[]{:S(2)}, u32[]{:S(2)}) %collective-permute-start.8) | collective-permute-done | bytes 327712 | tf_op jit(solution)/shard_map/ppermute | solution.py:153
  88.8 3.2 %collective-permute-start.14 = (f32[84,8,128]{2,1,0:T(8,128)}, f32[84,8,128]{2,1,0:T(8,128)S(1)}, u32[]{:S(2)}, u32[]{:S(2)}) collective-permute-start(f32[84,8,128]{2,1,0:T(8,128)} %get-tuple-element.25), channel_id=1, source_target_pairs={{0,48},{8,24},{1,49},{9,25},{2,50},{10,26},{3,51},{11,27},{4,52},{... | collective-permute-start | bytes 1032200 | tf_op jit(solution)/shard_map/ppermute | solution.py:153
  92.8 3.2 %collective-permute-start.20 = (f32[64,8,128]{2,1,0:T(8,128)S(1)}, f32[64,8,128]{2,1,0:T(8,128)}, u32[]{:S(2)}, u32[]{:S(2)}) collective-permute-start(f32[64,8,128]{2,1,0:T(8,128)S(1)} %get-tuple-element.27), channel_id=1, source_target_pairs={{0,192},{8,72},{1,193},{9,73},{2,194},{10,74},{3,195},{11,75},{4,1... | collective-permute-start | bytes 786440 | tf_op jit(solution)/shard_map/ppermute | solution.py:153
  96.0 3.4 %collective-permute-done.12 = f32[84,8,128]{2,1,0:T(8,128)S(1)} collective-permute-done((f32[84,8,128]{2,1,0:T(8,128)S(1)}, f32[84,8,128]{2,1,0:T(8,128)S(1)}, u32[]{:S(2)}, u32[]{:S(2)}) %collective-permute-start.12) | collective-permute-done | bytes 344096 | tf_op jit(solution)/shard_map/ppermute | solution.py:153
  100.3 1.8 %collective-permute-done.19 = f32[64,8,128]{2,1,0:T(8,128)} collective-permute-done((f32[64,8,128]{2,1,0:T(8,128)}, f32[64,8,128]{2,1,0:T(8,128)}, u32[]{:S(2)}, u32[]{:S(2)}) %collective-permute-start.19) | collective-permute-done | bytes 262176 | tf_op jit(solution)/shard_map/ppermute | solution.py:153
  103.2 5.8 %collective-permute-done.13 = f32[84,8,128]{2,1,0:T(8,128)S(1)} collective-permute-done((f32[84,8,128]{2,1,0:T(8,128)}, f32[84,8,128]{2,1,0:T(8,128)S(1)}, u32[]{:S(2)}, u32[]{:S(2)}) %collective-permute-start.13) | collective-permute-done | bytes 344096 | tf_op jit(solution)/shard_map/ppermute | solution.py:153
  109.1 2.0 %collective-permute-start.22 = (f32[32,8,128]{2,1,0:T(8,128)S(1)}, f32[32,8,128]{2,1,0:T(8,128)S(1)}, u32[]{:S(2)}, u32[]{:S(2)}) collective-permute-start(f32[32,8,128]{2,1,0:T(8,128)S(1)} %pad_maximum_fusion.2), channel_id=1, source_target_pairs={{0,2},{8,14},{1,3},{9,15},{2,4},{10,8},{3,5},{11,9},{4,6},{12,10},... | collective-permute-start | bytes 393224 | tf_op jit(solution)/shard_map/ppermute | solution.py:153
  111.0 2.3 %collective-permute-start.21 = (f32[32,8,128]{2,1,0:T(8,128)S(1)}, f32[32,8,128]{2,1,0:T(8,128)S(1)}, u32[]{:S(2)}, u32[]{:S(2)}) collective-permute-start(f32[32,8,128]{2,1,0:T(8,128)S(1)} %pad_maximum_fusion.1), channel_id=1, source_target_pairs={{0,6},{8,10},{1,7},{9,11},{2,0},{10,12},{3,1},{11,13},{4,2},{12,14... | collective-permute-start | bytes 393224 | tf_op jit(solution)/shard_map/ppermute | solution.py:153
  114.1 2.4 %collective-permute-done.22 = f32[32,8,128]{2,1,0:T(8,128)S(1)} collective-permute-done((f32[32,8,128]{2,1,0:T(8,128)S(1)}, f32[32,8,128]{2,1,0:T(8,128)S(1)}, u32[]{:S(2)}, u32[]{:S(2)}) %collective-permute-start.22) | collective-permute-done | bytes 131104 | tf_op jit(solution)/shard_map/ppermute | solution.py:153
  117.7 3.1 %collective-permute-start.25 = (f32[16,8,128]{2,1,0:T(8,128)S(1)}, f32[16,8,128]{2,1,0:T(8,128)S(1)}, u32[]{:S(2)}, u32[]{:S(2)}) collective-permute-start(f32[16,8,128]{2,1,0:T(8,128)S(1)} %get-tuple-element.31), channel_id=1, source_target_pairs={{0,7},{8,9},{1,0},{9,10},{2,1},{10,11},{3,2},{11,12},{4,3},{12,13}... | collective-permute-start | bytes 196616 | tf_op jit(solution)/shard_map/ppermute | solution.py:153
  120.8 2.9 %collective-permute-start.24 = (f32[16,8,128]{2,1,0:T(8,128)S(1)}, f32[16,8,128]{2,1,0:T(8,128)S(1)}, u32[]{:S(2)}, u32[]{:S(2)}) collective-permute-start(f32[16,8,128]{2,1,0:T(8,128)S(1)} %get-tuple-element.30), channel_id=1, source_target_pairs={{0,1},{8,15},{1,2},{9,8},{2,3},{10,9},{3,4},{11,10},{4,5},{12,11},... | collective-permute-start | bytes 196616 | tf_op jit(solution)/shard_map/ppermute | solution.py:153
  123.8 1.4 collective-permute-start.23
  125.9 4.4 %collective-permute-done.23 = f32[16,8,128]{2,1,0:T(8,128)S(1)} collective-permute-done((f32[16,8,128]{2,1,0:T(8,128)S(1)}, f32[16,8,128]{2,1,0:T(8,128)S(1)}, u32[]{:S(2)}, u32[]{:S(2)}) %collective-permute-start.23) | collective-permute-done | bytes 65568 | tf_op jit(solution)/shard_map/ppermute | solution.py:153
  130.8 5.9 %collective-permute-done.27 = f32[26,8,128]{2,1,0:T(8,128)S(1)} collective-permute-done((f32[26,8,128]{2,1,0:T(8,128)S(1)}, f32[26,8,128]{2,1,0:T(8,128)S(1)}, u32[]{:S(2)}, u32[]{:S(2)}) %collective-permute-start.27) | collective-permute-done | bytes 106528 | tf_op jit(solution)/shard_map/ppermute | solution.py:153
  (58 shorter events, 20.2 us)
Async XLA Ops:
  22.0 4.9 %collective-permute-start = (f32[592,8,128]{2,1,0:T(8,128)}, f32[592,8,128]{2,1,0:T(8,128)S(1)}, u32[]{:S(2)}, u32[]{:S(2)}) collective-permute-start(f32[592,8,128]{2,1,0:T(8,128)} %get-tuple-element.9), channel_id=1, source_target_pairs={{0,8},{8,0},{1,9},{9,1},{2,10},{10,2},{3,11},{11,3},{4,12},{12,4},... | collective-permute-start | bytes 7274504 | tf_op jit(solution)/shard_map/ppermute | solution.py:153
  28.1 13.7 %collective-permute-start.2 = (f32[2096,8,128]{2,1,0:T(8,128)}, f32[2096,8,128]{2,1,0:T(8,128)S(1)}, u32[]{:S(2)}, u32[]{:S(2)}) collective-permute-start(f32[2096,8,128]{2,1,0:T(8,128)} %after.1), channel_id=1, source_target_pairs={{0,8},{8,0},{1,9},{9,1},{2,10},{10,2},{3,11},{11,3},{4,12},{12,4},... | collective-permute-start | bytes 25755656 | tf_op jit(solution)/shard_map/ppermute | solution.py:153
  30.1 16.5 %collective-permute-start.15 = (f32[256,8,128]{2,1,0:T(8,128)S(1)}, f32[256,8,128]{2,1,0:T(8,128)S(1)}, u32[]{:S(2)}, u32[]{:S(2)}) collective-permute-start(f32[256,8,128]{2,1,0:T(8,128)S(1)} %get-tuple-element.23), channel_id=1, source_target_pairs={{0,16},{8,56},{1,17},{9,57},{2,18},{10,58},{3,19},{11,59},{4,20},{... | collective-permute-start | bytes 3145736 | tf_op jit(solution)/shard_map/ppermute | solution.py:153
  31.8 16.0 %collective-permute-start.1 = (f32[256,8,128]{2,1,0:T(8,128)S(1)}, f32[256,8,128]{2,1,0:T(8,128)S(1)}, u32[]{:S(2)}, u32[]{:S(2)}) collective-permute-start(f32[256,8,128]{2,1,0:T(8,128)S(1)} %get-tuple-element.24), channel_id=1, source_target_pairs={{0,64},{8,200},{1,65},{9,201},{2,66},{10,202},{3,67},{11,203},{4,6... | collective-permute-start | bytes 3145736 | tf_op jit(solution)/shard_map/ppermute | solution.py:153
  34.3 7.2 %collective-permute-start.5 = (f32[80,8,128]{2,1,0:T(8,128)S(1)}, f32[80,8,128]{2,1,0:T(8,128)S(1)}, u32[]{:S(2)}, u32[]{:S(2)}) collective-permute-start(f32[80,8,128]{2,1,0:T(8,128)S(1)} %slice_add_fusion.15), channel_id=1, source_target_pairs={{0,1},{8,15},{1,2},{9,8},{2,3},{10,9},{3,4},{11,10},{4,5},{12,11},... | collective-permute-start | bytes 983048 | tf_op jit(solution)/shard_map/ppermute | solution.py:153
  43.0 11.4 %collective-permute-start.9 = (f32[80,8,128]{2,1,0:T(8,128)S(1)}, f32[80,8,128]{2,1,0:T(8,128)S(1)}, u32[]{:S(2)}, u32[]{:S(2)}) collective-permute-start(f32[80,8,128]{2,1,0:T(8,128)S(1)} %get-tuple-element.21), channel_id=1, source_target_pairs={{0,7},{8,9},{1,0},{9,10},{2,1},{10,11},{3,2},{11,12},{4,3},{12,13}... | collective-permute-start | bytes 983048 | tf_op jit(solution)/shard_map/ppermute | solution.py:153
  46.6 10.4 %collective-permute-start.6 = (f32[80,8,128]{2,1,0:T(8,128)S(1)}, f32[80,8,128]{2,1,0:T(8,128)S(1)}, u32[]{:S(2)}, u32[]{:S(2)}) collective-permute-start(f32[80,8,128]{2,1,0:T(8,128)S(1)} %get-tuple-element.22), channel_id=1, source_target_pairs={{0,1},{8,15},{1,2},{9,8},{2,3},{10,9},{3,4},{11,10},{4,5},{12,11},... | collective-permute-start | bytes 983048 | tf_op jit(solution)/shard_map/ppermute | solution.py:153
  50.5 27.0 %collective-permute-start.16 = (f32[256,8,128]{2,1,0:T(8,128)S(1)}, f32[256,8,128]{2,1,0:T(8,128)S(1)}, u32[]{:S(2)}, u32[]{:S(2)}) collective-permute-start(f32[256,8,128]{2,1,0:T(8,128)S(1)} %get-tuple-element.14), channel_id=1, source_target_pairs={{0,16},{8,56},{1,17},{9,57},{2,18},{10,58},{3,19},{11,59},{4,20},{... | collective-permute-start | bytes 3145736 | tf_op jit(solution)/shard_map/ppermute | solution.py:153
  52.1 27.5 %collective-permute-start.17 = (f32[256,8,128]{2,1,0:T(8,128)S(1)}, f32[256,8,128]{2,1,0:T(8,128)S(1)}, u32[]{:S(2)}, u32[]{:S(2)}) collective-permute-start(f32[256,8,128]{2,1,0:T(8,128)S(1)} %get-tuple-element.13), channel_id=1, source_target_pairs={{0,48},{8,24},{1,49},{9,25},{2,50},{10,26},{3,51},{11,27},{4,52},{... | collective-permute-start | bytes 3145736 | tf_op jit(solution)/shard_map/ppermute | solution.py:153
  53.8 27.1 %collective-permute-start.3 = (f32[256,8,128]{2,1,0:T(8,128)S(1)}, f32[256,8,128]{2,1,0:T(8,128)S(1)}, u32[]{:S(2)}, u32[]{:S(2)}) collective-permute-start(f32[256,8,128]{2,1,0:T(8,128)S(1)} %get-tuple-element.16), channel_id=1, source_target_pairs={{0,64},{8,200},{1,65},{9,201},{2,66},{10,202},{3,67},{11,203},{4,6... | collective-permute-start | bytes 3145736 | tf_op jit(solution)/shard_map/ppermute | solution.py:153
  54.4 26.5 %collective-permute-start.4 = (f32[256,8,128]{2,1,0:T(8,128)S(1)}, f32[256,8,128]{2,1,0:T(8,128)S(1)}, u32[]{:S(2)}, u32[]{:S(2)}) collective-permute-start(f32[256,8,128]{2,1,0:T(8,128)S(1)} %get-tuple-element.15), channel_id=1, source_target_pairs={{0,192},{8,72},{1,193},{9,73},{2,194},{10,74},{3,195},{11,75},{4,1... | collective-permute-start | bytes 3145736 | tf_op jit(solution)/shard_map/ppermute | solution.py:153
  58.2 7.2 %collective-permute-start.10 = (f32[80,8,128]{2,1,0:T(8,128)S(1)}, f32[80,8,128]{2,1,0:T(8,128)S(1)}, u32[]{:S(2)}, u32[]{:S(2)}) collective-permute-start(f32[80,8,128]{2,1,0:T(8,128)S(1)} %get-tuple-element.19), channel_id=1, source_target_pairs={{0,7},{8,9},{1,0},{9,10},{2,1},{10,11},{3,2},{11,12},{4,3},{12,13}... | collective-permute-start | bytes 983048 | tf_op jit(solution)/shard_map/ppermute | solution.py:153
  65.4 8.9 %collective-permute-start.7 = (f32[80,8,128]{2,1,0:T(8,128)S(1)}, f32[80,8,128]{2,1,0:T(8,128)S(1)}, u32[]{:S(2)}, u32[]{:S(2)}) collective-permute-start(f32[80,8,128]{2,1,0:T(8,128)S(1)} %get-tuple-element.20), channel_id=1, source_target_pairs={{0,1},{8,15},{1,2},{9,8},{2,3},{10,9},{3,4},{11,10},{4,5},{12,11},... | collective-permute-start | bytes 983048 | tf_op jit(solution)/shard_map/ppermute | solution.py:153
  75.5 11.5 %collective-permute-start.8 = (f32[80,8,128]{2,1,0:T(8,128)S(1)}, f32[80,8,128]{2,1,0:T(8,128)S(1)}, u32[]{:S(2)}, u32[]{:S(2)}) collective-permute-start(f32[80,8,128]{2,1,0:T(8,128)S(1)} %get-tuple-element.18), channel_id=1, source_target_pairs={{0,1},{8,15},{1,2},{9,8},{2,3},{10,9},{3,4},{11,10},{4,5},{12,11},... | collective-permute-start | bytes 983048 | tf_op jit(solution)/shard_map/ppermute | solution.py:153
  77.5 9.5 %collective-permute-start.11 = (f32[80,8,128]{2,1,0:T(8,128)S(1)}, f32[80,8,128]{2,1,0:T(8,128)S(1)}, u32[]{:S(2)}, u32[]{:S(2)}) collective-permute-start(f32[80,8,128]{2,1,0:T(8,128)S(1)} %get-tuple-element.17), channel_id=1, source_target_pairs={{0,7},{8,9},{1,0},{9,10},{2,1},{10,11},{3,2},{11,12},{4,3},{12,13}... | collective-permute-start | bytes 983048 | tf_op jit(solution)/shard_map/ppermute | solution.py:153
  83.1 9.0 %collective-permute-start.18 = (f32[64,8,128]{2,1,0:T(8,128)S(1)}, f32[64,8,128]{2,1,0:T(8,128)S(1)}, u32[]{:S(2)}, u32[]{:S(2)}) collective-permute-start(f32[64,8,128]{2,1,0:T(8,128)S(1)} %slice.247), channel_id=1, source_target_pairs={{0,64},{8,200},{1,65},{9,201},{2,66},{10,202},{3,67},{11,203},{4,6... | collective-permute-start | bytes 786440 | tf_op jit(solution)/shard_map/ppermute | solution.py:153
  88.8 10.7 %collective-permute-start.12 = (f32[84,8,128]{2,1,0:T(8,128)S(1)}, f32[84,8,128]{2,1,0:T(8,128)S(1)}, u32[]{:S(2)}, u32[]{:S(2)}) collective-permute-start(f32[84,8,128]{2,1,0:T(8,128)S(1)} %get-tuple-element.26), channel_id=1, source_target_pairs={{0,16},{8,56},{1,17},{9,57},{2,18},{10,58},{3,19},{11,59},{4,20},{... | collective-permute-start | bytes 1032200 | tf_op jit(solution)/shard_map/ppermute | solution.py:153
  88.8 14.4 %collective-permute-start.14 = (f32[84,8,128]{2,1,0:T(8,128)}, f32[84,8,128]{2,1,0:T(8,128)S(1)}, u32[]{:S(2)}, u32[]{:S(2)}) collective-permute-start(f32[84,8,128]{2,1,0:T(8,128)} %get-tuple-element.25), channel_id=1, source_target_pairs={{0,48},{8,24},{1,49},{9,25},{2,50},{10,26},{3,51},{11,27},{4,52},{... | collective-permute-start | bytes 1032200 | tf_op jit(solution)/shard_map/ppermute | solution.py:153
  92.8 9.3 %collective-permute-start.19 = (f32[64,8,128]{2,1,0:T(8,128)}, f32[64,8,128]{2,1,0:T(8,128)}, u32[]{:S(2)}, u32[]{:S(2)}) collective-permute-start(f32[64,8,128]{2,1,0:T(8,128)} %get-tuple-element.28), channel_id=1, source_target_pairs={{0,64},{8,200},{1,65},{9,201},{2,66},{10,202},{3,67},{11,203},{4,6... | collective-permute-start | bytes 786440 | tf_op jit(solution)/shard_map/ppermute | solution.py:153
  92.8 9.3 %collective-permute-start.20 = (f32[64,8,128]{2,1,0:T(8,128)S(1)}, f32[64,8,128]{2,1,0:T(8,128)}, u32[]{:S(2)}, u32[]{:S(2)}) collective-permute-start(f32[64,8,128]{2,1,0:T(8,128)S(1)} %get-tuple-element.27), channel_id=1, source_target_pairs={{0,192},{8,72},{1,193},{9,73},{2,194},{10,74},{3,195},{11,75},{4,1... | collective-permute-start | bytes 786440 | tf_op jit(solution)/shard_map/ppermute | solution.py:153
  100.3 8.7 %collective-permute-start.13 = (f32[84,8,128]{2,1,0:T(8,128)}, f32[84,8,128]{2,1,0:T(8,128)S(1)}, u32[]{:S(2)}, u32[]{:S(2)}) collective-permute-start(f32[84,8,128]{2,1,0:T(8,128)} %fusion.10), channel_id=1, source_target_pairs={{0,16},{8,56},{1,17},{9,57},{2,18},{10,58},{3,19},{11,59},{4,20},{... | collective-permute-start | bytes 1032200 | tf_op jit(solution)/shard_map/ppermute | solution.py:153
  109.1 7.4 %collective-permute-start.22 = (f32[32,8,128]{2,1,0:T(8,128)S(1)}, f32[32,8,128]{2,1,0:T(8,128)S(1)}, u32[]{:S(2)}, u32[]{:S(2)}) collective-permute-start(f32[32,8,128]{2,1,0:T(8,128)S(1)} %pad_maximum_fusion.2), channel_id=1, source_target_pairs={{0,2},{8,14},{1,3},{9,15},{2,4},{10,8},{3,5},{11,9},{4,6},{12,10},... | collective-permute-start | bytes 393224 | tf_op jit(solution)/shard_map/ppermute | solution.py:153
  111.0 6.6 %collective-permute-start.21 = (f32[32,8,128]{2,1,0:T(8,128)S(1)}, f32[32,8,128]{2,1,0:T(8,128)S(1)}, u32[]{:S(2)}, u32[]{:S(2)}) collective-permute-start(f32[32,8,128]{2,1,0:T(8,128)S(1)} %pad_maximum_fusion.1), channel_id=1, source_target_pairs={{0,6},{8,10},{1,7},{9,11},{2,0},{10,12},{3,1},{11,13},{4,2},{12,14... | collective-permute-start | bytes 393224 | tf_op jit(solution)/shard_map/ppermute | solution.py:153
  113.4 11.8 %collective-permute-start.26 = (f32[10,8,128]{2,1,0:T(8,128)S(1)}, f32[10,8,128]{2,1,0:T(8,128)S(1)}, u32[]{:S(2)}, u32[]{:S(2)}) collective-permute-start(f32[10,8,128]{2,1,0:T(8,128)S(1)} %dynamic-slice_bitcast_fusion), channel_id=1, source_target_pairs={{0,64},{8,72},{1,65},{9,73},{2,66},{10,74},{3,67},{11,75},{4,68},{... | collective-permute-start | bytes 122888 | tf_op jit(solution)/shard_map/ppermute | solution.py:153
  117.7 8.2 %collective-permute-start.25 = (f32[16,8,128]{2,1,0:T(8,128)S(1)}, f32[16,8,128]{2,1,0:T(8,128)S(1)}, u32[]{:S(2)}, u32[]{:S(2)}) collective-permute-start(f32[16,8,128]{2,1,0:T(8,128)S(1)} %get-tuple-element.31), channel_id=1, source_target_pairs={{0,7},{8,9},{1,0},{9,10},{2,1},{10,11},{3,2},{11,12},{4,3},{12,13}... | collective-permute-start | bytes 196616 | tf_op jit(solution)/shard_map/ppermute | solution.py:153
  120.8 5.1 %collective-permute-start.24 = (f32[16,8,128]{2,1,0:T(8,128)S(1)}, f32[16,8,128]{2,1,0:T(8,128)S(1)}, u32[]{:S(2)}, u32[]{:S(2)}) collective-permute-start(f32[16,8,128]{2,1,0:T(8,128)S(1)} %get-tuple-element.30), channel_id=1, source_target_pairs={{0,1},{8,15},{1,2},{9,8},{2,3},{10,9},{3,4},{11,10},{4,5},{12,11},... | collective-permute-start | bytes 196616 | tf_op jit(solution)/shard_map/ppermute | solution.py:153
  123.8 6.5 %collective-permute-start.23 = (f32[16,8,128]{2,1,0:T(8,128)S(1)}, f32[16,8,128]{2,1,0:T(8,128)S(1)}, u32[]{:S(2)}, u32[]{:S(2)}) collective-permute-start(f32[16,8,128]{2,1,0:T(8,128)S(1)} %get-tuple-element.29), channel_id=1, source_target_pairs={{0,2},{8,14},{1,3},{9,15},{2,4},{10,8},{3,5},{11,9},{4,6},{12,10},... | collective-permute-start | bytes 196616 | tf_op jit(solution)/shard_map/ppermute | solution.py:153
  130.4 6.3 %collective-permute-start.27 = (f32[26,8,128]{2,1,0:T(8,128)S(1)}, f32[26,8,128]{2,1,0:T(8,128)S(1)}, u32[]{:S(2)}, u32[]{:S(2)}) collective-permute-start(f32[26,8,128]{2,1,0:T(8,128)S(1)} %pad_maximum_fusion.3), channel_id=1, source_target_pairs={{0,128},{8,136},{1,129},{9,137},{2,130},{10,138},{3,131},{11,139},... | collective-permute-start | bytes 319496 | tf_op jit(solution)/shard_map/ppermute | solution.py:153

commit v3 on v2

--- a/solution.py
+++ b/solution.py
@@ -46,47 +46,50 @@
     ]
     fetch_h[0].start()
     fetch_c.start()
-    for i in range(1, steps):
-        fetch_h[i].start()
     fetch_c.wait()
     flat = acc.reshape(5376 * 8, 128)
     parts = acc.reshape(16, 8, 2, 21, 8, 128)
 
-    def copy_out(src, row, mine):
+    def put(src, row, dst, base):
         count = 1
         for n in src.shape[:-2]:
             count *= n
-
-        def put(dst, base):
-            to = dst.at[pl.ds(row - base, count)].reshape(src.shape)
-            pltpu.make_async_copy(src, to, sem).start()
-
-        pl.when(mine)(lambda: put(keep, 0))
-        pl.when(jnp.logical_not(mine) & (row < CUT))(lambda: put(send1, 0))
-        pl.when(jnp.logical_not(mine) & (row >= CUT))(lambda: put(send2, CUT))
+        to = dst.at[pl.ds(row - base, count)].reshape(src.shape)
+        pltpu.make_async_copy(src, to, sem).start()
 
     def block_out(b):
         c2, y2, xl = b % 2, b // 2 % 4, b // 8
         sign = 1 - 2 * c2
-        mine = core == c2
         rely = lax.rem(sign * (y2 - y) + 4, 4)
+        copies = []
         for xh in range(2):
             relx = lax.rem(sign * (2 * xh + xl - x) + 4, 4)
             to_x = pick("x", relx, 4) + rely * (8 * RX)
             to_y = pick("y", rely, 4) + relx * (8 * RY)
-            copy_out(parts.at[b, :, xh, pl.ds(0, RX)], to_x, mine)
-            copy_out(parts.at[b, :, xh, pl.ds(RX, RY)], to_y, mine)
+            copies.append((parts.at[b, :, xh, pl.ds(0, RX)], to_x))
+            copies.append((parts.at[b, :, xh, pl.ds(RX, RY)], to_y))
         for z2 in range(8):
             relz = lax.rem(sign * (z2 - z) + 8, 8)
-            copy_out(
-                parts.at[b, z2, :, pl.ds(RX + RY, RZ)],
-                pick("z", relz, 8) + (rely * 4 + xl * 2) * RZ,
-                mine,
-            )
+            to_z = pick("z", relz, 8) + (rely * 4 + xl * 2) * RZ
+            copies.append((parts.at[b, z2, :, pl.ds(RX + RY, RZ)], to_z))
+
+        @pl.when(core == c2)
+        def _():
+            for src, row in copies:
+                put(src, row, keep, 0)
+
+        @pl.when(core != c2)
+        def _():
+            for src, row in copies:
+                pl.when(row < CUT)(lambda: put(src, row, send1, 0))
+                pl.when(row >= CUT)(lambda: put(src, row, send2, CUT))
 
     out = 0
     for i in range(steps):
         fetch_h[i].wait()
+        for ahead in (1, 2) if i == 0 else (i + 2,):
+            if ahead < steps:
+                fetch_h[ahead].start()
         for j in range(0, STEP, 256):
             prod = lax.dot_general(
                 h_buf[i, :, j : j + 256],

time: 138 us -> 135 us (0.978)
  Pallas kernels: 21.4 us -> 18.9 us
    pallas_call x1, Pallas kernels: 21.4 us -> 18.9 us  [local_grad(): pl.pallas_call(grad_kernel, out_shape=(shape(ROWS), shape(CUT), shape(ROW...]
  transfers between devices with their start and end apart: 28 -> 28, of which waited for: 18 -> 18; matrix products, arithmetic and copies ran while one was open for 11% -> 12% of each run, Pallas kernels for 0% -> 0%
where the time goes in v3:
time: 135 us
  waiting for transfers between devices  55.8 us (41%)
  starting transfers between devices  41.8 us (31%)
  Pallas kernels  18.9 us (14%)
  other arithmetic  17.7 us (13%)
    ppermute x28, waiting for transfers between devices, send(): return lax.ppermute(a, AXES, pairs)  55.8 us
    ppermute x28, starting transfers between devices, send(): return lax.ppermute(a, AXES, pairs)  41.8 us
    pallas_call x1, Pallas kernels, local_grad(): pl.pallas_call(grad_kernel, out_shape=(shape(ROWS), shape(CUT), shape(ROW...  18.9 us
    add x4, other arithmetic, own(): return keep[row:row + count] + got[row - base:row - base + count]  6.58 us
  transfers between devices with their start and end apart: 28, of which 18 were waited for; matrix products, arithmetic and copies ran while one was open for 12% of the time, Pallas kernels for 0%

profile of v3, /device:TPU:32, one launch (start us, length us, event | category | flops | bytes accessed | tf_op | source)
XLA Modules:
  0.0 135.0 jit_solution(13023735761315552478)
XLA Ops:
  0.6 18.9 %local_grad.1 = (f32[2688,8,128]{2,1,0:T(8,128)}, f32[592,8,128]{2,1,0:T(8,128)}, f32[2096,8,128]{2,1,0:T(8,128)}) custom-call(s32[4]{0:T(128)} %pad_add_fusion.where_ref, bf16[1024,5376]{1,0:T(8,128)(2,1)} %h_ref.1, bf16[1024,1024]{1,0:T(8,128)(2,1)} %c_ref.1), custom_call_target="tpu_custom_call" | custom-call | flops 11274289152 | bytes 35127296 | tf_op jit(solution)/shard_map/local_grad/pallas_call | solution.py:114
  19.6 4.8 %collective-permute-done = f32[592,8,128]{2,1,0:T(8,128)S(1)} collective-permute-done((f32[592,8,128]{2,1,0:T(8,128)}, f32[592,8,128]{2,1,0:T(8,128)S(1)}, u32[]{:S(2)}, u32[]{:S(2)}) %collective-permute-start) | collective-permute-done | bytes 2424864 | tf_op jit(solution)/shard_map/ppermute | solution.py:156
  25.8 1.8 %slice_add_fusion.3 = (f32[256,8,128]{2,1,0:T(8,128)S(1)}, f32[256,8,128]{2,1,0:T(8,128)S(1)}) fusion(f32[592,8,128]{2,1,0:T(8,128)S(1)} %collective-permute-done, f32[2688,8,128]{2,1,0:T(8,128)} %get-tuple-element.8), kind=kLoop, calls=%fused_computation.27 | loop fusion | flops 524288 | bytes 6291456 | tf_op jit(solution)/shard_map/add | solution.py:198
  27.6 1.7 %collective-permute-start.15 = (f32[256,8,128]{2,1,0:T(8,128)S(1)}, f32[256,8,128]{2,1,0:T(8,128)S(1)}, u32[]{:S(2)}, u32[]{:S(2)}) collective-permute-start(f32[256,8,128]{2,1,0:T(8,128)S(1)} %get-tuple-element.23), channel_id=1, source_target_pairs={{0,16},{8,56},{1,17},{9,57},{2,18},{10,58},{3,19},{11,59},{4,20},{... | collective-permute-start | bytes 3145736 | tf_op jit(solution)/shard_map/ppermute | solution.py:156
  29.3 1.5 %collective-permute-start.1 = (f32[256,8,128]{2,1,0:T(8,128)S(1)}, f32[256,8,128]{2,1,0:T(8,128)S(1)}, u32[]{:S(2)}, u32[]{:S(2)}) collective-permute-start(f32[256,8,128]{2,1,0:T(8,128)S(1)} %get-tuple-element.24), channel_id=1, source_target_pairs={{0,64},{8,200},{1,65},{9,201},{2,66},{10,202},{3,67},{11,203},{4,6... | collective-permute-start | bytes 3145736 | tf_op jit(solution)/shard_map/ppermute | solution.py:156
  31.8 2.0 %collective-permute-start.5 = (f32[80,8,128]{2,1,0:T(8,128)S(1)}, f32[80,8,128]{2,1,0:T(8,128)S(1)}, u32[]{:S(2)}, u32[]{:S(2)}) collective-permute-start(f32[80,8,128]{2,1,0:T(8,128)S(1)} %slice_add_fusion.15), channel_id=1, source_target_pairs={{0,1},{8,15},{1,2},{9,8},{2,3},{10,9},{3,4},{11,10},{4,5},{12,11},... | collective-permute-start | bytes 983048 | tf_op jit(solution)/shard_map/ppermute | solution.py:156
  33.8 5.2 %collective-permute-done.5 = f32[80,8,128]{2,1,0:T(8,128)S(1)} collective-permute-done((f32[80,8,128]{2,1,0:T(8,128)S(1)}, f32[80,8,128]{2,1,0:T(8,128)S(1)}, u32[]{:S(2)}, u32[]{:S(2)}) %collective-permute-start.5) | collective-permute-done | bytes 327712 | tf_op jit(solution)/shard_map/ppermute | solution.py:156
  40.5 3.6 %collective-permute-start.9 = (f32[80,8,128]{2,1,0:T(8,128)S(1)}, f32[80,8,128]{2,1,0:T(8,128)S(1)}, u32[]{:S(2)}, u32[]{:S(2)}) collective-permute-start(f32[80,8,128]{2,1,0:T(8,128)S(1)} %get-tuple-element.21), channel_id=1, source_target_pairs={{0,7},{8,9},{1,0},{9,10},{2,1},{10,11},{3,2},{11,12},{4,3},{12,13}... | collective-permute-start | bytes 983048 | tf_op jit(solution)/shard_map/ppermute | solution.py:156
  45.3 2.7 %slice_add_fusion.1 = (f32[256,8,128]{2,1,0:T(8,128)S(1)}, f32[256,8,128]{2,1,0:T(8,128)S(1)}, f32[256,8,128]{2,1,0:T(8,128)S(1)}, f32[256,8,128]{2,1,0:T(8,128)S(1)}) fusion(f32[2096,8,128]{2,1,0:T(8,128)S(1)} %collective-permute-done.2, f32[2688,8,128]{2,1,0:T(8,128)} %get-tuple-element.8, f32[256,8,128]{2,1,0:T(8,128)S(1)} %collective-permute-done.15, ...), kind=kLoop, calls=%fused_computation.24 | loop fusion | flops 1572864 | bytes 14680064 | tf_op jit(solution)/shard_map/add | solution.py:198
  48.0 1.6 %collective-permute-start.16 = (f32[256,8,128]{2,1,0:T(8,128)S(1)}, f32[256,8,128]{2,1,0:T(8,128)S(1)}, u32[]{:S(2)}, u32[]{:S(2)}) collective-permute-start(f32[256,8,128]{2,1,0:T(8,128)S(1)} %get-tuple-element.14), channel_id=1, source_target_pairs={{0,16},{8,56},{1,17},{9,57},{2,18},{10,58},{3,19},{11,59},{4,20},{... | collective-permute-start | bytes 3145736 | tf_op jit(solution)/shard_map/ppermute | solution.py:156
  49.6 1.7 %collective-permute-start.17 = (f32[256,8,128]{2,1,0:T(8,128)S(1)}, f32[256,8,128]{2,1,0:T(8,128)S(1)}, u32[]{:S(2)}, u32[]{:S(2)}) collective-permute-start(f32[256,8,128]{2,1,0:T(8,128)S(1)} %get-tuple-element.13), channel_id=1, source_target_pairs={{0,48},{8,24},{1,49},{9,25},{2,50},{10,26},{3,51},{11,27},{4,52},{... | collective-permute-start | bytes 3145736 | tf_op jit(solution)/shard_map/ppermute | solution.py:156
  51.9 2.6 %collective-permute-start.4 = (f32[256,8,128]{2,1,0:T(8,128)S(1)}, f32[256,8,128]{2,1,0:T(8,128)S(1)}, u32[]{:S(2)}, u32[]{:S(2)}) collective-permute-start(f32[256,8,128]{2,1,0:T(8,128)S(1)} %get-tuple-element.15), channel_id=1, source_target_pairs={{0,192},{8,72},{1,193},{9,73},{2,194},{10,74},{3,195},{11,75},{4,1... | collective-permute-start | bytes 3145736 | tf_op jit(solution)/shard_map/ppermute | solution.py:156
  55.7 2.6 %collective-permute-start.10 = (f32[80,8,128]{2,1,0:T(8,128)S(1)}, f32[80,8,128]{2,1,0:T(8,128)S(1)}, u32[]{:S(2)}, u32[]{:S(2)}) collective-permute-start(f32[80,8,128]{2,1,0:T(8,128)S(1)} %get-tuple-element.19), channel_id=1, source_target_pairs={{0,7},{8,9},{1,0},{9,10},{2,1},{10,11},{3,2},{11,12},{4,3},{12,13}... | collective-permute-start | bytes 983048 | tf_op jit(solution)/shard_map/ppermute | solution.py:156
  58.3 4.6 %collective-permute-done.10 = f32[80,8,128]{2,1,0:T(8,128)S(1)} collective-permute-done((f32[80,8,128]{2,1,0:T(8,128)S(1)}, f32[80,8,128]{2,1,0:T(8,128)S(1)}, u32[]{:S(2)}, u32[]{:S(2)}) %collective-permute-start.10) | collective-permute-done | bytes 327712 | tf_op jit(solution)/shard_map/ppermute | solution.py:156
  62.9 1.9 %collective-permute-start.7 = (f32[80,8,128]{2,1,0:T(8,128)S(1)}, f32[80,8,128]{2,1,0:T(8,128)S(1)}, u32[]{:S(2)}, u32[]{:S(2)}) collective-permute-start(f32[80,8,128]{2,1,0:T(8,128)S(1)} %get-tuple-element.20), channel_id=1, source_target_pairs={{0,1},{8,15},{1,2},{9,8},{2,3},{10,9},{3,4},{11,10},{4,5},{12,11},... | collective-permute-start | bytes 983048 | tf_op jit(solution)/shard_map/ppermute | solution.py:156
  64.8 7.0 %collective-permute-done.7 = f32[80,8,128]{2,1,0:T(8,128)S(1)} collective-permute-done((f32[80,8,128]{2,1,0:T(8,128)S(1)}, f32[80,8,128]{2,1,0:T(8,128)S(1)}, u32[]{:S(2)}, u32[]{:S(2)}) %collective-permute-start.7) | collective-permute-done | bytes 327712 | tf_op jit(solution)/shard_map/ppermute | solution.py:156
  75.0 1.9 %collective-permute-start.11 = (f32[80,8,128]{2,1,0:T(8,128)S(1)}, f32[80,8,128]{2,1,0:T(8,128)S(1)}, u32[]{:S(2)}, u32[]{:S(2)}) collective-permute-start(f32[80,8,128]{2,1,0:T(8,128)S(1)} %get-tuple-element.17), channel_id=1, source_target_pairs={{0,7},{8,9},{1,0},{9,10},{2,1},{10,11},{3,2},{11,12},{4,3},{12,13}... | collective-permute-start | bytes 983048 | tf_op jit(solution)/shard_map/ppermute | solution.py:156
  76.9 1.5 %collective-permute-done.3 = f32[256,8,128]{2,1,0:T(8,128)S(1)} collective-permute-done((f32[256,8,128]{2,1,0:T(8,128)S(1)}, f32[256,8,128]{2,1,0:T(8,128)S(1)}, u32[]{:S(2)}, u32[]{:S(2)}) %collective-permute-start.3) | collective-permute-done | bytes 1048608 | tf_op jit(solution)/shard_map/ppermute | solution.py:156
  78.4 2.2 %fusion = (f32[256,8,128]{2,1,0:T(8,128)S(1)}, f32[256,8,128]{2,1,0:T(8,128)S(1)}) fusion(f32[2096,8,128]{2,1,0:T(8,128)S(1)} %collective-permute-done.2, f32[2688,8,128]{2,1,0:T(8,128)} %get-tuple-element.8, f32[256,8,128]{2,1,0:T(8,128)S(1)} %collective-permute-done.16, f32[256,8,128]{2,1,0:T(8,128)S(1)} %collective-permute-done.17, ...), kind=kLoop, calls=%fused_computation.23 | loop fusion | flops 1572864 | bytes 10485760 | tf_op jit(solution)/shard_map/add | solution.py:204
  80.7 3.8 %collective-permute-done.8 = f32[80,8,128]{2,1,0:T(8,128)S(1)} collective-permute-done((f32[80,8,128]{2,1,0:T(8,128)S(1)}, f32[80,8,128]{2,1,0:T(8,128)S(1)}, u32[]{:S(2)}, u32[]{:S(2)}) %collective-permute-start.8) | collective-permute-done | bytes 327712 | tf_op jit(solution)/shard_map/ppermute | solution.py:156
  86.3 3.2 %collective-permute-start.14 = (f32[84,8,128]{2,1,0:T(8,128)}, f32[84,8,128]{2,1,0:T(8,128)S(1)}, u32[]{:S(2)}, u32[]{:S(2)}) collective-permute-start(f32[84,8,128]{2,1,0:T(8,128)} %get-tuple-element.25), channel_id=1, source_target_pairs={{0,48},{8,24},{1,49},{9,25},{2,50},{10,26},{3,51},{11,27},{4,52},{... | collective-permute-start | bytes 1032200 | tf_op jit(solution)/shard_map/ppermute | solution.py:156
  90.3 3.2 %collective-permute-start.20 = (f32[64,8,128]{2,1,0:T(8,128)S(1)}, f32[64,8,128]{2,1,0:T(8,128)}, u32[]{:S(2)}, u32[]{:S(2)}) collective-permute-start(f32[64,8,128]{2,1,0:T(8,128)S(1)} %get-tuple-element.27), channel_id=1, source_target_pairs={{0,192},{8,72},{1,193},{9,73},{2,194},{10,74},{3,195},{11,75},{4,1... | collective-permute-start | bytes 786440 | tf_op jit(solution)/shard_map/ppermute | solution.py:156
  93.5 3.4 %collective-permute-done.12 = f32[84,8,128]{2,1,0:T(8,128)S(1)} collective-permute-done((f32[84,8,128]{2,1,0:T(8,128)S(1)}, f32[84,8,128]{2,1,0:T(8,128)S(1)}, u32[]{:S(2)}, u32[]{:S(2)}) %collective-permute-start.12) | collective-permute-done | bytes 344096 | tf_op jit(solution)/shard_map/ppermute | solution.py:156
  97.8 1.8 %collective-permute-done.19 = f32[64,8,128]{2,1,0:T(8,128)} collective-permute-done((f32[64,8,128]{2,1,0:T(8,128)}, f32[64,8,128]{2,1,0:T(8,128)}, u32[]{:S(2)}, u32[]{:S(2)}) %collective-permute-start.19) | collective-permute-done | bytes 262176 | tf_op jit(solution)/shard_map/ppermute | solution.py:156
  100.7 5.8 %collective-permute-done.13 = f32[84,8,128]{2,1,0:T(8,128)S(1)} collective-permute-done((f32[84,8,128]{2,1,0:T(8,128)}, f32[84,8,128]{2,1,0:T(8,128)S(1)}, u32[]{:S(2)}, u32[]{:S(2)}) %collective-permute-start.13) | collective-permute-done | bytes 344096 | tf_op jit(solution)/shard_map/ppermute | solution.py:156
  106.6 2.0 %collective-permute-start.22 = (f32[32,8,128]{2,1,0:T(8,128)S(1)}, f32[32,8,128]{2,1,0:T(8,128)S(1)}, u32[]{:S(2)}, u32[]{:S(2)}) collective-permute-start(f32[32,8,128]{2,1,0:T(8,128)S(1)} %pad_maximum_fusion.2), channel_id=1, source_target_pairs={{0,2},{8,14},{1,3},{9,15},{2,4},{10,8},{3,5},{11,9},{4,6},{12,10},... | collective-permute-start | bytes 393224 | tf_op jit(solution)/shard_map/ppermute | solution.py:156
  108.6 2.3 %collective-permute-start.21 = (f32[32,8,128]{2,1,0:T(8,128)S(1)}, f32[32,8,128]{2,1,0:T(8,128)S(1)}, u32[]{:S(2)}, u32[]{:S(2)}) collective-permute-start(f32[32,8,128]{2,1,0:T(8,128)S(1)} %pad_maximum_fusion.1), channel_id=1, source_target_pairs={{0,6},{8,10},{1,7},{9,11},{2,0},{10,12},{3,1},{11,13},{4,2},{12,14... | collective-permute-start | bytes 393224 | tf_op jit(solution)/shard_map/ppermute | solution.py:156
  111.6 2.6 %collective-permute-done.22 = f32[32,8,128]{2,1,0:T(8,128)S(1)} collective-permute-done((f32[32,8,128]{2,1,0:T(8,128)S(1)}, f32[32,8,128]{2,1,0:T(8,128)S(1)}, u32[]{:S(2)}, u32[]{:S(2)}) %collective-permute-start.22) | collective-permute-done | bytes 131104 | tf_op jit(solution)/shard_map/ppermute | solution.py:156
  115.2 3.1 %collective-permute-start.25 = (f32[16,8,128]{2,1,0:T(8,128)S(1)}, f32[16,8,128]{2,1,0:T(8,128)S(1)}, u32[]{:S(2)}, u32[]{:S(2)}) collective-permute-start(f32[16,8,128]{2,1,0:T(8,128)S(1)} %get-tuple-element.31), channel_id=1, source_target_pairs={{0,7},{8,9},{1,0},{9,10},{2,1},{10,11},{3,2},{11,12},{4,3},{12,13}... | collective-permute-start | bytes 196616 | tf_op jit(solution)/shard_map/ppermute | solution.py:156
  118.4 2.9 %collective-permute-start.24 = (f32[16,8,128]{2,1,0:T(8,128)S(1)}, f32[16,8,128]{2,1,0:T(8,128)S(1)}, u32[]{:S(2)}, u32[]{:S(2)}) collective-permute-start(f32[16,8,128]{2,1,0:T(8,128)S(1)} %get-tuple-element.30), channel_id=1, source_target_pairs={{0,1},{8,15},{1,2},{9,8},{2,3},{10,9},{3,4},{11,10},{4,5},{12,11},... | collective-permute-start | bytes 196616 | tf_op jit(solution)/shard_map/ppermute | solution.py:156
  123.5 4.4 %collective-permute-done.23 = f32[16,8,128]{2,1,0:T(8,128)S(1)} collective-permute-done((f32[16,8,128]{2,1,0:T(8,128)S(1)}, f32[16,8,128]{2,1,0:T(8,128)S(1)}, u32[]{:S(2)}, u32[]{:S(2)}) %collective-permute-start.23) | collective-permute-done | bytes 65568 | tf_op jit(solution)/shard_map/ppermute | solution.py:156
  128.3 5.9 %collective-permute-done.27 = f32[26,8,128]{2,1,0:T(8,128)S(1)} collective-permute-done((f32[26,8,128]{2,1,0:T(8,128)S(1)}, f32[26,8,128]{2,1,0:T(8,128)S(1)}, u32[]{:S(2)}, u32[]{:S(2)}) %collective-permute-start.27) | collective-permute-done | bytes 106528 | tf_op jit(solution)/shard_map/ppermute | solution.py:156
  (58 shorter events, 20.0 us)
Async XLA Ops:
  19.5 4.9 %collective-permute-start = (f32[592,8,128]{2,1,0:T(8,128)}, f32[592,8,128]{2,1,0:T(8,128)S(1)}, u32[]{:S(2)}, u32[]{:S(2)}) collective-permute-start(f32[592,8,128]{2,1,0:T(8,128)} %get-tuple-element.9), channel_id=1, source_target_pairs={{0,8},{8,0},{1,9},{9,1},{2,10},{10,2},{3,11},{11,3},{4,12},{12,4},... | collective-permute-start | bytes 7274504 | tf_op jit(solution)/shard_map/ppermute | solution.py:156
  25.6 13.7 %collective-permute-start.2 = (f32[2096,8,128]{2,1,0:T(8,128)}, f32[2096,8,128]{2,1,0:T(8,128)S(1)}, u32[]{:S(2)}, u32[]{:S(2)}) collective-permute-start(f32[2096,8,128]{2,1,0:T(8,128)} %after.1), channel_id=1, source_target_pairs={{0,8},{8,0},{1,9},{9,1},{2,10},{10,2},{3,11},{11,3},{4,12},{12,4},... | collective-permute-start | bytes 25755656 | tf_op jit(solution)/shard_map/ppermute | solution.py:156
  27.6 16.5 %collective-permute-start.15 = (f32[256,8,128]{2,1,0:T(8,128)S(1)}, f32[256,8,128]{2,1,0:T(8,128)S(1)}, u32[]{:S(2)}, u32[]{:S(2)}) collective-permute-start(f32[256,8,128]{2,1,0:T(8,128)S(1)} %get-tuple-element.23), channel_id=1, source_target_pairs={{0,16},{8,56},{1,17},{9,57},{2,18},{10,58},{3,19},{11,59},{4,20},{... | collective-permute-start | bytes 3145736 | tf_op jit(solution)/shard_map/ppermute | solution.py:156
  29.3 16.0 %collective-permute-start.1 = (f32[256,8,128]{2,1,0:T(8,128)S(1)}, f32[256,8,128]{2,1,0:T(8,128)S(1)}, u32[]{:S(2)}, u32[]{:S(2)}) collective-permute-start(f32[256,8,128]{2,1,0:T(8,128)S(1)} %get-tuple-element.24), channel_id=1, source_target_pairs={{0,64},{8,200},{1,65},{9,201},{2,66},{10,202},{3,67},{11,203},{4,6... | collective-permute-start | bytes 3145736 | tf_op jit(solution)/shard_map/ppermute | solution.py:156
  31.8 7.2 %collective-permute-start.5 = (f32[80,8,128]{2,1,0:T(8,128)S(1)}, f32[80,8,128]{2,1,0:T(8,128)S(1)}, u32[]{:S(2)}, u32[]{:S(2)}) collective-permute-start(f32[80,8,128]{2,1,0:T(8,128)S(1)} %slice_add_fusion.15), channel_id=1, source_target_pairs={{0,1},{8,15},{1,2},{9,8},{2,3},{10,9},{3,4},{11,10},{4,5},{12,11},... | collective-permute-start | bytes 983048 | tf_op jit(solution)/shard_map/ppermute | solution.py:156
  40.5 11.4 %collective-permute-start.9 = (f32[80,8,128]{2,1,0:T(8,128)S(1)}, f32[80,8,128]{2,1,0:T(8,128)S(1)}, u32[]{:S(2)}, u32[]{:S(2)}) collective-permute-start(f32[80,8,128]{2,1,0:T(8,128)S(1)} %get-tuple-element.21), channel_id=1, source_target_pairs={{0,7},{8,9},{1,0},{9,10},{2,1},{10,11},{3,2},{11,12},{4,3},{12,13}... | collective-permute-start | bytes 983048 | tf_op jit(solution)/shard_map/ppermute | solution.py:156
  44.1 10.4 %collective-permute-start.6 = (f32[80,8,128]{2,1,0:T(8,128)S(1)}, f32[80,8,128]{2,1,0:T(8,128)S(1)}, u32[]{:S(2)}, u32[]{:S(2)}) collective-permute-start(f32[80,8,128]{2,1,0:T(8,128)S(1)} %get-tuple-element.22), channel_id=1, source_target_pairs={{0,1},{8,15},{1,2},{9,8},{2,3},{10,9},{3,4},{11,10},{4,5},{12,11},... | collective-permute-start | bytes 983048 | tf_op jit(solution)/shard_map/ppermute | solution.py:156
  48.0 27.0 %collective-permute-start.16 = (f32[256,8,128]{2,1,0:T(8,128)S(1)}, f32[256,8,128]{2,1,0:T(8,128)S(1)}, u32[]{:S(2)}, u32[]{:S(2)}) collective-permute-start(f32[256,8,128]{2,1,0:T(8,128)S(1)} %get-tuple-element.14), channel_id=1, source_target_pairs={{0,16},{8,56},{1,17},{9,57},{2,18},{10,58},{3,19},{11,59},{4,20},{... | collective-permute-start | bytes 3145736 | tf_op jit(solution)/shard_map/ppermute | solution.py:156
  49.6 27.3 %collective-permute-start.17 = (f32[256,8,128]{2,1,0:T(8,128)S(1)}, f32[256,8,128]{2,1,0:T(8,128)S(1)}, u32[]{:S(2)}, u32[]{:S(2)}) collective-permute-start(f32[256,8,128]{2,1,0:T(8,128)S(1)} %get-tuple-element.13), channel_id=1, source_target_pairs={{0,48},{8,24},{1,49},{9,25},{2,50},{10,26},{3,51},{11,27},{4,52},{... | collective-permute-start | bytes 3145736 | tf_op jit(solution)/shard_map/ppermute | solution.py:156
  51.3 27.1 %collective-permute-start.3 = (f32[256,8,128]{2,1,0:T(8,128)S(1)}, f32[256,8,128]{2,1,0:T(8,128)S(1)}, u32[]{:S(2)}, u32[]{:S(2)}) collective-permute-start(f32[256,8,128]{2,1,0:T(8,128)S(1)} %get-tuple-element.16), channel_id=1, source_target_pairs={{0,64},{8,200},{1,65},{9,201},{2,66},{10,202},{3,67},{11,203},{4,6... | collective-permute-start | bytes 3145736 | tf_op jit(solution)/shard_map/ppermute | solution.py:156
  51.9 26.5 %collective-permute-start.4 = (f32[256,8,128]{2,1,0:T(8,128)S(1)}, f32[256,8,128]{2,1,0:T(8,128)S(1)}, u32[]{:S(2)}, u32[]{:S(2)}) collective-permute-start(f32[256,8,128]{2,1,0:T(8,128)S(1)} %get-tuple-element.15), channel_id=1, source_target_pairs={{0,192},{8,72},{1,193},{9,73},{2,194},{10,74},{3,195},{11,75},{4,1... | collective-permute-start | bytes 3145736 | tf_op jit(solution)/shard_map/ppermute | solution.py:156
  55.7 7.2 %collective-permute-start.10 = (f32[80,8,128]{2,1,0:T(8,128)S(1)}, f32[80,8,128]{2,1,0:T(8,128)S(1)}, u32[]{:S(2)}, u32[]{:S(2)}) collective-permute-start(f32[80,8,128]{2,1,0:T(8,128)S(1)} %get-tuple-element.19), channel_id=1, source_target_pairs={{0,7},{8,9},{1,0},{9,10},{2,1},{10,11},{3,2},{11,12},{4,3},{12,13}... | collective-permute-start | bytes 983048 | tf_op jit(solution)/shard_map/ppermute | solution.py:156
  62.9 8.9 %collective-permute-start.7 = (f32[80,8,128]{2,1,0:T(8,128)S(1)}, f32[80,8,128]{2,1,0:T(8,128)S(1)}, u32[]{:S(2)}, u32[]{:S(2)}) collective-permute-start(f32[80,8,128]{2,1,0:T(8,128)S(1)} %get-tuple-element.20), channel_id=1, source_target_pairs={{0,1},{8,15},{1,2},{9,8},{2,3},{10,9},{3,4},{11,10},{4,5},{12,11},... | collective-permute-start | bytes 983048 | tf_op jit(solution)/shard_map/ppermute | solution.py:156
  73.0 11.5 %collective-permute-start.8 = (f32[80,8,128]{2,1,0:T(8,128)S(1)}, f32[80,8,128]{2,1,0:T(8,128)S(1)}, u32[]{:S(2)}, u32[]{:S(2)}) collective-permute-start(f32[80,8,128]{2,1,0:T(8,128)S(1)} %get-tuple-element.18), channel_id=1, source_target_pairs={{0,1},{8,15},{1,2},{9,8},{2,3},{10,9},{3,4},{11,10},{4,5},{12,11},... | collective-permute-start | bytes 983048 | tf_op jit(solution)/shard_map/ppermute | solution.py:156
  75.0 9.5 %collective-permute-start.11 = (f32[80,8,128]{2,1,0:T(8,128)S(1)}, f32[80,8,128]{2,1,0:T(8,128)S(1)}, u32[]{:S(2)}, u32[]{:S(2)}) collective-permute-start(f32[80,8,128]{2,1,0:T(8,128)S(1)} %get-tuple-element.17), channel_id=1, source_target_pairs={{0,7},{8,9},{1,0},{9,10},{2,1},{10,11},{3,2},{11,12},{4,3},{12,13}... | collective-permute-start | bytes 983048 | tf_op jit(solution)/shard_map/ppermute | solution.py:156
  80.6 9.0 %collective-permute-start.18 = (f32[64,8,128]{2,1,0:T(8,128)S(1)}, f32[64,8,128]{2,1,0:T(8,128)S(1)}, u32[]{:S(2)}, u32[]{:S(2)}) collective-permute-start(f32[64,8,128]{2,1,0:T(8,128)S(1)} %slice.247), channel_id=1, source_target_pairs={{0,64},{8,200},{1,65},{9,201},{2,66},{10,202},{3,67},{11,203},{4,6... | collective-permute-start | bytes 786440 | tf_op jit(solution)/shard_map/ppermute | solution.py:156
  86.3 10.7 %collective-permute-start.12 = (f32[84,8,128]{2,1,0:T(8,128)S(1)}, f32[84,8,128]{2,1,0:T(8,128)S(1)}, u32[]{:S(2)}, u32[]{:S(2)}) collective-permute-start(f32[84,8,128]{2,1,0:T(8,128)S(1)} %get-tuple-element.26), channel_id=1, source_target_pairs={{0,16},{8,56},{1,17},{9,57},{2,18},{10,58},{3,19},{11,59},{4,20},{... | collective-permute-start | bytes 1032200 | tf_op jit(solution)/shard_map/ppermute | solution.py:156
  86.3 14.4 %collective-permute-start.14 = (f32[84,8,128]{2,1,0:T(8,128)}, f32[84,8,128]{2,1,0:T(8,128)S(1)}, u32[]{:S(2)}, u32[]{:S(2)}) collective-permute-start(f32[84,8,128]{2,1,0:T(8,128)} %get-tuple-element.25), channel_id=1, source_target_pairs={{0,48},{8,24},{1,49},{9,25},{2,50},{10,26},{3,51},{11,27},{4,52},{... | collective-permute-start | bytes 1032200 | tf_op jit(solution)/shard_map/ppermute | solution.py:156
  90.3 9.3 %collective-permute-start.19 = (f32[64,8,128]{2,1,0:T(8,128)}, f32[64,8,128]{2,1,0:T(8,128)}, u32[]{:S(2)}, u32[]{:S(2)}) collective-permute-start(f32[64,8,128]{2,1,0:T(8,128)} %get-tuple-element.28), channel_id=1, source_target_pairs={{0,64},{8,200},{1,65},{9,201},{2,66},{10,202},{3,67},{11,203},{4,6... | collective-permute-start | bytes 786440 | tf_op jit(solution)/shard_map/ppermute | solution.py:156
  90.3 9.3 %collective-permute-start.20 = (f32[64,8,128]{2,1,0:T(8,128)S(1)}, f32[64,8,128]{2,1,0:T(8,128)}, u32[]{:S(2)}, u32[]{:S(2)}) collective-permute-start(f32[64,8,128]{2,1,0:T(8,128)S(1)} %get-tuple-element.27), channel_id=1, source_target_pairs={{0,192},{8,72},{1,193},{9,73},{2,194},{10,74},{3,195},{11,75},{4,1... | collective-permute-start | bytes 786440 | tf_op jit(solution)/shard_map/ppermute | solution.py:156
  97.8 8.7 %collective-permute-start.13 = (f32[84,8,128]{2,1,0:T(8,128)}, f32[84,8,128]{2,1,0:T(8,128)S(1)}, u32[]{:S(2)}, u32[]{:S(2)}) collective-permute-start(f32[84,8,128]{2,1,0:T(8,128)} %fusion.10), channel_id=1, source_target_pairs={{0,16},{8,56},{1,17},{9,57},{2,18},{10,58},{3,19},{11,59},{4,20},{... | collective-permute-start | bytes 1032200 | tf_op jit(solution)/shard_map/ppermute | solution.py:156
  106.6 7.6 %collective-permute-start.22 = (f32[32,8,128]{2,1,0:T(8,128)S(1)}, f32[32,8,128]{2,1,0:T(8,128)S(1)}, u32[]{:S(2)}, u32[]{:S(2)}) collective-permute-start(f32[32,8,128]{2,1,0:T(8,128)S(1)} %pad_maximum_fusion.2), channel_id=1, source_target_pairs={{0,2},{8,14},{1,3},{9,15},{2,4},{10,8},{3,5},{11,9},{4,6},{12,10},... | collective-permute-start | bytes 393224 | tf_op jit(solution)/shard_map/ppermute | solution.py:156
  108.6 6.7 %collective-permute-start.21 = (f32[32,8,128]{2,1,0:T(8,128)S(1)}, f32[32,8,128]{2,1,0:T(8,128)S(1)}, u32[]{:S(2)}, u32[]{:S(2)}) collective-permute-start(f32[32,8,128]{2,1,0:T(8,128)S(1)} %pad_maximum_fusion.1), channel_id=1, source_target_pairs={{0,6},{8,10},{1,7},{9,11},{2,0},{10,12},{3,1},{11,13},{4,2},{12,14... | collective-permute-start | bytes 393224 | tf_op jit(solution)/shard_map/ppermute | solution.py:156
  110.9 11.8 %collective-permute-start.26 = (f32[10,8,128]{2,1,0:T(8,128)S(1)}, f32[10,8,128]{2,1,0:T(8,128)S(1)}, u32[]{:S(2)}, u32[]{:S(2)}) collective-permute-start(f32[10,8,128]{2,1,0:T(8,128)S(1)} %dynamic-slice_bitcast_fusion), channel_id=1, source_target_pairs={{0,64},{8,72},{1,65},{9,73},{2,66},{10,74},{3,67},{11,75},{4,68},{... | collective-permute-start | bytes 122888 | tf_op jit(solution)/shard_map/ppermute | solution.py:156
  115.2 8.2 %collective-permute-start.25 = (f32[16,8,128]{2,1,0:T(8,128)S(1)}, f32[16,8,128]{2,1,0:T(8,128)S(1)}, u32[]{:S(2)}, u32[]{:S(2)}) collective-permute-start(f32[16,8,128]{2,1,0:T(8,128)S(1)} %get-tuple-element.31), channel_id=1, source_target_pairs={{0,7},{8,9},{1,0},{9,10},{2,1},{10,11},{3,2},{11,12},{4,3},{12,13}... | collective-permute-start | bytes 196616 | tf_op jit(solution)/shard_map/ppermute | solution.py:156
  118.4 5.1 %collective-permute-start.24 = (f32[16,8,128]{2,1,0:T(8,128)S(1)}, f32[16,8,128]{2,1,0:T(8,128)S(1)}, u32[]{:S(2)}, u32[]{:S(2)}) collective-permute-start(f32[16,8,128]{2,1,0:T(8,128)S(1)} %get-tuple-element.30), channel_id=1, source_target_pairs={{0,1},{8,15},{1,2},{9,8},{2,3},{10,9},{3,4},{11,10},{4,5},{12,11},... | collective-permute-start | bytes 196616 | tf_op jit(solution)/shard_map/ppermute | solution.py:156
  121.3 6.5 %collective-permute-start.23 = (f32[16,8,128]{2,1,0:T(8,128)S(1)}, f32[16,8,128]{2,1,0:T(8,128)S(1)}, u32[]{:S(2)}, u32[]{:S(2)}) collective-permute-start(f32[16,8,128]{2,1,0:T(8,128)S(1)} %get-tuple-element.29), channel_id=1, source_target_pairs={{0,2},{8,14},{1,3},{9,15},{2,4},{10,8},{3,5},{11,9},{4,6},{12,10},... | collective-permute-start | bytes 196616 | tf_op jit(solution)/shard_map/ppermute | solution.py:156
  127.9 6.3 %collective-permute-start.27 = (f32[26,8,128]{2,1,0:T(8,128)S(1)}, f32[26,8,128]{2,1,0:T(8,128)S(1)}, u32[]{:S(2)}, u32[]{:S(2)}) collective-permute-start(f32[26,8,128]{2,1,0:T(8,128)S(1)} %pad_maximum_fusion.3), channel_id=1, source_target_pairs={{0,128},{8,136},{1,129},{9,137},{2,130},{10,138},{3,131},{11,139},... | collective-permute-start | bytes 319496 | tf_op jit(solution)/shard_map/ppermute | solution.py:156
